TPU v7x, 32 devices: a whole 2x2x4 slice. The times are simulated.
32 devices in a mesh: dp: 8 (over z, x), row: 2 (over y), col: 2 (over core).
Axes of the slice: x: 2, y: 2, z: 4, core: 2. Of those that a mesh axis runs over, the one named last changes fastest.
Arguments:
- tokens: bfloat16 [8192, 768], P(('dp', 'row')), may hold values from -6 to 6
- grad_out: bfloat16 [8192, 768], P(('dp', 'row')), may hold values from -6 to 6
- routes: int32 [8192, 1], P(('dp', 'row')), may hold values from 0 to 1; in each aligned block of 512 rows (0 to 511, 512 to 1023, ...) at most 512 rows name the same one
- norm1_gain: bfloat16 [768], replicated, may hold values from 0.099609375 to 1.8984375
- w_query: bfloat16 [768, 768], P('row', 'col'), may hold values from -0.21875 to 0.21875
- w_key: bfloat16 [768, 768], P('row', 'col'), may hold values from -0.21875 to 0.21875
- w_value: bfloat16 [768, 768], P('row', 'col'), may hold values from -0.21875 to 0.21875
- w_output: bfloat16 [768, 768], P('row', 'col'), may hold values from -0.875 to 0.875
- rel_table: bfloat16 [32, 12], replicated, may hold values from -4 to 4
- rel_bucket: int32 [2047], replicated, may hold values from 0 to 31
- norm2_gain: bfloat16 [768], replicated, may hold values from 0.099609375 to 1.8984375
- router: bfloat16 [768, 2], replicated, may hold values from -0.15625 to 0.15625
- w_in: bfloat16 [2, 768, 3072], P('row', None, 'col'), may hold values from -0.21875 to 0.21875
- w_out: bfloat16 [2, 768, 3072], P('row', None, 'col'), may hold values from -0.625 to 0.625
Outputs:
- output: bfloat16 [8192, 768], P(('dp', 'row'))
- grad_tokens: float32 [8192, 768], P(('dp', 'row'))
- grad_norm1: float32 [768], P(('dp', 'row'))
- grad_w_query: float32 [768, 768], P(('dp', 'row'), 'col')
- grad_w_key: float32 [768, 768], P(('dp', 'row'), 'col')
- grad_w_value: float32 [768, 768], P(('dp', 'row'), 'col')
- grad_w_output: float32 [768, 768], P(('dp', 'row'), 'col')
- grad_table: float32 [32, 12], P(None, 'col')
- grad_norm2: float32 [768], P(('dp', 'row'))
- grad_router: float32 [768, 2], P(('dp', 'row'))
- grad_w_in: float32 [2, 768, 3072], P('row', 'dp', 'col')
- grad_w_out: float32 [2, 768, 3072], P('row', 'dp', 'col')
Inputs may be any that keep to these rules, and one draw needn't show every extreme that they name: `routes`: within the rows of one device (512 consecutive tokens) no expert is named by more than 512 tokens, and in some such blocks one expert is named by exactly 512.
All inputs are finite; a program needn't handle non-finite values.
Results may differ from a plain program's by a relative error of at most 0.015.
Values may be sent and summed in bfloat16 or wider, within the bound.
No kernel may reach another device: no remote copies, remote signals or barrier semaphores. Data moves between devices by JAX's collectives and lax.ppermute only.
A program may use at most 192 MiB of HBM per device.

v0:
```python
import jax
import jax.numpy as jnp
from jax import lax
from jax.sharding import PartitionSpec as P

H = 12
NBUCKET = 32


EPS = 1e-06
SCALE = 0.125
HIGHEST = lax.Precision.HIGHEST
NARROW = jnp.bfloat16
WIDE = jnp.float32


def gelu_tanh(values):
    return jax.nn.gelu(values, approximate=True)


def norm_forward(rows, gain):
    inverse = lax.rsqrt(jnp.mean(rows * rows, axis=-1, keepdims=True) + EPS)
    return (rows * inverse * gain, inverse)


def norm_backward(rows, inverse, gain, grad_normed):
    scaled = grad_normed * gain
    grad_rows = inverse * scaled - rows * inverse**3 * jnp.mean(
        scaled * rows, axis=-1, keepdims=True
    )
    return (grad_rows, jnp.sum(grad_normed * rows * inverse, axis=0))


def contract_rows(left, right):
    return lax.dot_general(left, right, (((0,), (0,)), ((), ())), preferred_element_type=WIDE)


def contract_cols(left, right):
    return lax.dot_general(left, right, (((1,), (1,)), ((), ())), preferred_element_type=WIDE)


def split_heads(matrix, heads):
    return matrix.reshape(matrix.shape[0], heads, -1).transpose(1, 0, 2)


def join_heads(stacked):
    return stacked.transpose(1, 0, 2).reshape(stacked.shape[1], -1)


def diagonal_sums(block):
    heads, height, breadth = block.shape
    shifted = jnp.pad(block, ((0, 0), (0, 0), (height, 0))).reshape(
        heads, height * (height + breadth)
    )
    shifted = jnp.pad(shifted, ((0, 0), (0, height))).reshape(heads, height, height + breadth + 1)
    totals = jnp.sum(shifted, axis=1, dtype=WIDE)
    return totals[:, 1 : height + breadth]


def bias_block(offsets, query_start, key_start, queries, keys, seq_len):
    heads = offsets.shape[0]
    begin = key_start - query_start + seq_len - queries
    window = lax.dynamic_slice_in_dim(offsets, begin, queries + keys - 1, 1)
    period = queries + keys
    padded = jnp.pad(window, ((0, 0), (0, 1)))
    spread = jnp.broadcast_to(padded[:, None, :], (heads, queries, period)).reshape(
        heads, queries * period
    )
    skewed = spread[:, : queries * (period - 1)].reshape(heads, queries, period - 1)
    return skewed[:, :, queries - 1 : queries - 1 + keys]


def batch_scores(query_heads, key_heads, bias):
    return (
        SCALE * jnp.einsum("hqd,hkd->hqk", query_heads, key_heads, preferred_element_type=WIDE)
        + bias
    )


def local(
    tokens,
    grad_out,
    routes,
    norm1_gain,
    w_query,
    w_key,
    w_value,
    w_output,
    rel_table,
    rel_bucket,
    norm2_gain,
    router,
    w_in,
    w_out,
):
    tok_rows, width = tokens.shape
    seq_len = tok_rows * lax.axis_size("row")
    heads = H // lax.axis_size("col")
    row_start = lax.axis_index("row") * tok_rows
    tokens_wide = tokens.astype(WIDE)
    gain_one = norm1_gain.astype(WIDE)
    normed, inverse_one = norm_forward(tokens_wide, gain_one)
    normed_low = normed.astype(NARROW)
    query_weight, key_weight, value_weight, output_weight = (
        lax.all_gather(w_query, "row", axis=0, tiled=True),
        lax.all_gather(w_key, "row", axis=0, tiled=True),
        lax.all_gather(w_value, "row", axis=0, tiled=True),
        lax.all_gather(w_output, "row", axis=0, tiled=True),
    )
    query = jnp.dot(normed_low, query_weight, preferred_element_type=WIDE).astype(NARROW)
    key = jnp.dot(normed_low, key_weight, preferred_element_type=WIDE).astype(NARROW)
    value = jnp.dot(normed_low, value_weight, preferred_element_type=WIDE).astype(NARROW)
    keys_all, values_all = (
        lax.all_gather(key, "row", axis=0, tiled=True),
        lax.all_gather(value, "row", axis=0, tiled=True),
    )
    bucket_hot = (rel_bucket[None, :] == jnp.arange(NBUCKET, dtype=jnp.int32)[:, None]).astype(WIDE)
    table_local = lax.dynamic_slice_in_dim(
        rel_table.astype(WIDE), lax.axis_index("col") * heads, heads, 1
    )
    offsets = jnp.dot(table_local.T, bucket_hot, precision=HIGHEST)
    bias = bias_block(offsets, row_start, 0, tok_rows, seq_len, seq_len)
    query_heads = split_heads(query, heads)
    key_heads = split_heads(keys_all, heads)
    value_heads = split_heads(values_all, heads)
    scores = batch_scores(query_heads, key_heads, bias)
    ceiling = jnp.max(scores, axis=2, keepdims=True)
    raised = jnp.exp(scores - ceiling)
    summed = jnp.sum(raised, axis=2, keepdims=True)
    attended_heads = jnp.einsum(
        "hqk,hkd->hqd", (raised / summed).astype(NARROW), value_heads, preferred_element_type=WIDE
    )
    log_total = ceiling[:, :, 0] + jnp.log(summed[:, :, 0])
    attended = join_heads(attended_heads).astype(NARROW)
    branch = lax.psum(contract_cols(attended, output_weight), "col")
    hidden = tokens_wide + branch
    gain_two = norm2_gain.astype(WIDE)
    hn, inverse_two = norm_forward(hidden, gain_two)
    router_wide = router.astype(WIDE)
    gate_probs = jax.nn.softmax(jnp.dot(hn, router_wide, precision=HIGHEST), axis=-1)
    n_exp = router.shape[1]
    capacity = 2 * tok_rows // n_exp
    expert_ids = routes[:, 0]
    one_hot_int = (expert_ids[:, None] == jnp.arange(n_exp, dtype=jnp.int32)[None, :]).astype(
        jnp.int32
    )
    one_hot = one_hot_int.astype(WIDE)
    gate = jnp.sum(gate_probs * one_hot, axis=1)
    rank_own = jnp.sum((jnp.cumsum(one_hot_int, axis=0) - 1) * one_hot_int, axis=1)
    slot_ids = expert_ids * capacity + rank_own
    grad_wide = grad_out.astype(WIDE)
    send_rows = hn.astype(NARROW)
    send_grads = (gate[:, None] * grad_wide).astype(NARROW)
    box_rows = (
        jnp.zeros((n_exp * capacity, width), NARROW)
        .at[slot_ids]
        .set(send_rows)
        .reshape(n_exp, capacity, width)
    )
    box_grads = (
        jnp.zeros((n_exp * capacity, width), NARROW)
        .at[slot_ids]
        .set(send_grads)
        .reshape(n_exp, capacity, width)
    )
    got_rows, got_grads = (
        lax.all_to_all(box_rows, "row", split_axis=0, concat_axis=0, tiled=True),
        lax.all_to_all(box_grads, "row", split_axis=0, concat_axis=0, tiled=True),
    )
    expert_in = got_rows.reshape(-1, width)
    expert_grad = got_grads.reshape(-1, width)
    weight_in = w_in[0]
    weight_out = w_out[0]
    pre = jnp.dot(expert_in, weight_in, preferred_element_type=WIDE)
    act, act_back = jax.vjp(gelu_tanh, pre)
    act_low = act.astype(NARROW)
    out_part = contract_cols(act_low, weight_out)
    grad_act = jnp.dot(expert_grad, weight_out, preferred_element_type=WIDE)
    grad_pre = act_back(grad_act)[0].astype(NARROW)
    rows_part = contract_cols(grad_pre, weight_in)
    grad_weight_in = contract_rows(expert_in, grad_pre)
    grad_weight_out = contract_rows(expert_grad, act_low)
    out_sum, rows_sum = lax.psum((out_part, rows_part), "col")
    back_out, back_rows = (
        lax.all_to_all(
            out_sum.astype(NARROW).reshape(n_exp, capacity, width),
            "row",
            split_axis=0,
            concat_axis=0,
            tiled=True,
        ),
        lax.all_to_all(
            rows_sum.astype(NARROW).reshape(n_exp, capacity, width),
            "row",
            split_axis=0,
            concat_axis=0,
            tiled=True,
        ),
    )
    expert_out = back_out.reshape(-1, width)[slot_ids].astype(WIDE)
    grad_rows = back_rows.reshape(-1, width)[slot_ids].astype(WIDE)
    output = (hidden + gate[:, None] * expert_out).astype(NARROW)
    grad_in_shard, grad_out_shard = (
        lax.psum_scatter(
            grad_weight_in.astype(jnp.bfloat16), "dp", scatter_dimension=0, tiled=True
        ).astype(jnp.float32),
        lax.psum_scatter(
            grad_weight_out.astype(jnp.bfloat16), "dp", scatter_dimension=0, tiled=True
        ).astype(jnp.float32),
    )
    grad_gate = jnp.sum(grad_wide * expert_out, axis=1)
    grad_logits = (grad_gate * gate)[:, None] * (one_hot - gate_probs)
    grad_router = jnp.dot(hn.T, grad_logits, precision=HIGHEST)
    grad_hn = grad_rows + jnp.dot(grad_logits, router_wide.T, precision=HIGHEST)
    grad_hidden_norm, grad_gain_two = norm_backward(hidden, inverse_two, gain_two, grad_hn)
    grad_hidden = grad_wide + grad_hidden_norm
    grad_branch = grad_hidden.astype(NARROW)
    grad_w_output = contract_rows(grad_branch, attended)
    grad_attended = jnp.dot(grad_branch, output_weight, preferred_element_type=WIDE).astype(NARROW)
    grad_heads = split_heads(grad_attended, heads)
    diagonal_start = seq_len - row_start - tok_rows
    shares = jnp.exp(batch_scores(query_heads, key_heads, bias) - log_total[:, :, None])
    grad_shares = jnp.einsum("hqd,hkd->hqk", grad_heads, value_heads, preferred_element_type=WIDE)
    deltas = jnp.sum(shares * grad_shares, axis=2)
    grad_scores = (shares * (grad_shares - deltas[:, :, None])).astype(NARROW)
    grad_query_heads = SCALE * jnp.einsum(
        "hqk,hkd->hqd", grad_scores, key_heads, preferred_element_type=WIDE
    )
    diagonals = diagonal_sums(grad_scores)
    bucket_window = lax.dynamic_slice_in_dim(bucket_hot, diagonal_start, tok_rows + seq_len - 1, 1)
    table_part = jnp.dot(bucket_window, diagonals.T, precision=HIGHEST)
    grad_key_heads = SCALE * jnp.einsum(
        "hqk,hqd->hkd", grad_scores, query_heads, preferred_element_type=WIDE
    )
    grad_value_heads = jnp.einsum(
        "hqk,hqd->hkd", shares.astype(NARROW), grad_heads, preferred_element_type=WIDE
    )
    grad_key, grad_value = (
        lax.psum_scatter(
            join_heads(grad_key_heads).astype(jnp.bfloat16), "row", scatter_dimension=0, tiled=True
        ).astype(jnp.float32),
        lax.psum_scatter(
            join_heads(grad_value_heads).astype(jnp.bfloat16),
            "row",
            scatter_dimension=0,
            tiled=True,
        ).astype(jnp.float32),
    )
    grad_query = join_heads(grad_query_heads).astype(NARROW)
    grad_key_low = grad_key.astype(NARROW)
    grad_value_low = grad_value.astype(NARROW)
    grad_w_query = contract_rows(normed_low, grad_query)
    grad_w_key = contract_rows(normed_low, grad_key_low)
    grad_w_value = contract_rows(normed_low, grad_value_low)
    normed_part = (
        contract_cols(grad_query, query_weight)
        + contract_cols(grad_key_low, key_weight)
        + contract_cols(grad_value_low, value_weight)
    )
    grad_normed = lax.psum(normed_part.astype(jnp.bfloat16), "col").astype(jnp.float32)
    grad_tokens_norm, grad_gain_one = norm_backward(tokens_wide, inverse_one, gain_one, grad_normed)
    grad_tokens = grad_hidden + grad_tokens_norm
    grad_table = lax.psum(table_part, ("dp", "row"))
    (
        grads_query,
        grads_key,
        grads_value,
        grads_output,
        grads_gain_one,
        grads_gain_two,
        grads_router,
    ) = (
        lax.psum_scatter(grad_w_query, ("dp", "row"), scatter_dimension=0, tiled=True),
        lax.psum_scatter(grad_w_key, ("dp", "row"), scatter_dimension=0, tiled=True),
        lax.psum_scatter(grad_w_value, ("dp", "row"), scatter_dimension=0, tiled=True),
        lax.psum_scatter(grad_w_output, ("dp", "row"), scatter_dimension=0, tiled=True),
        lax.psum_scatter(grad_gain_one, ("dp", "row"), scatter_dimension=0, tiled=True),
        lax.psum_scatter(grad_gain_two, ("dp", "row"), scatter_dimension=0, tiled=True),
        lax.psum_scatter(grad_router, ("dp", "row"), scatter_dimension=0, tiled=True),
    )
    return (
        output,
        grad_tokens,
        grads_gain_one,
        grads_query,
        grads_key,
        grads_value,
        grads_output,
        grad_table,
        grads_gain_two,
        grads_router,
        grad_in_shard[None],
        grad_out_shard[None],
    )


def solution(mesh):
    in_specs = (
        P(("dp", "row"), None),
        P(("dp", "row"), None),
        P(("dp", "row"), None),
        P(),
        P("row", "col"),
        P("row", "col"),
        P("row", "col"),
        P("row", "col"),
        P(),
        P(),
        P(),
        P(),
        P("row", None, "col"),
        P("row", None, "col"),
    )
    out_specs = (
        P(("dp", "row"), None),
        P(("dp", "row"), None),
        P(("dp", "row")),
        P(("dp", "row"), "col"),
        P(("dp", "row"), "col"),
        P(("dp", "row"), "col"),
        P(("dp", "row"), "col"),
        P(None, "col"),
        P(("dp", "row")),
        P(("dp", "row"), None),
        P("row", "dp", "col"),
        P("row", "dp", "col"),
    )
    return jax.shard_map(local, mesh=mesh, in_specs=in_specs, out_specs=out_specs, check_vma=False)
```

profile of v0, /device:TPU:0, one launch (start us, length us, event | category | flops | bytes accessed | tf_op | source)
XLA Modules:
  0.0 1586.9 jit_solution(18387220609619074117)
XLA Ops:
  10.1 10.9 all_gather.18
  21.0 9.1 all_gather.19
  31.4 10.2 all_gather.20
  52.9 8.6 all_gather.22
  63.8 8.6 all_gather.23
  72.6 8.9 broadcast_bitcast_fusion
  81.5 18.2 %copy.34 = f32[1,6,512,1536]{3,1,2,0:T(8,128)S(1)} copy(f32[1,6,512,1536]{3,2,1,0:T(8,128)} %broadcast_bitcast_fusion) | data formatting | bytes 37748736
  108.3 391.5 %while.2 = (u32[]{:T(128)}, f32[1,6,785920]{2,1,0:T(8,128)}, f32[4715520]{0:T(1024)}, u32[]{}, f32[]{:T(128)}, /*index=5*/u32[]{}, u32[]{}, u32[]{}) while((u32[]{:T(128)}, f32[1,6,785920]{2,1,0:T(8,128)}, f32[4715520]{0:T(1024)}, u32[]{}, f32[]{:T(128)}, /*index=5*/u32[]{}, u32[]{}, u32[]{}) %tuple.40), condition=%wide.cond, body=%wide.body.sunk | while | flops 9 | bytes 12574921
  108.8 37.0 %dynamic-slice_reduce_fusion.4 = f32[785920]{0:T(1024)} fusion(f32[]{:T(128)} %broadcast.187, f32[1,6,785920]{2,1,0:T(8,128)} %get-tuple-element.115, u32[]{:T(128)S(6)} %multiply.52, u32[]{:T(128)S(6)} %multiply.53), kind=kLoop, calls=%fused_computation.133.clone.1 | loop fusion | bytes 6287372
  145.8 27.8 %dynamic-update-slice.4 = f32[4715520]{0:T(1024)} dynamic-update-slice(f32[4715520]{0:T(1024)} %get-tuple-element.108, f32[785920]{0:T(1024)} %dynamic-slice_reduce_fusion.4, u32[]{:T(128)S(6)} %add.194) | dynamic-update-slice | bytes 6287364
  174.1 37.0 %dynamic-slice_reduce_fusion.4 = f32[785920]{0:T(1024)} fusion(f32[]{:T(128)} %broadcast.187, f32[1,6,785920]{2,1,0:T(8,128)} %get-tuple-element.115, u32[]{:T(128)S(6)} %multiply.52, u32[]{:T(128)S(6)} %multiply.53), kind=kLoop, calls=%fused_computation.133.clone.1 | loop fusion | bytes 6287372
  211.1 27.8 %dynamic-update-slice.4 = f32[4715520]{0:T(1024)} dynamic-update-slice(f32[4715520]{0:T(1024)} %get-tuple-element.108, f32[785920]{0:T(1024)} %dynamic-slice_reduce_fusion.4, u32[]{:T(128)S(6)} %add.194) | dynamic-update-slice | bytes 6287364
  239.4 37.0 %dynamic-slice_reduce_fusion.4 = f32[785920]{0:T(1024)} fusion(f32[]{:T(128)} %broadcast.187, f32[1,6,785920]{2,1,0:T(8,128)} %get-tuple-element.115, u32[]{:T(128)S(6)} %multiply.52, u32[]{:T(128)S(6)} %multiply.53), kind=kLoop, calls=%fused_computation.133.clone.1 | loop fusion | bytes 6287372
  276.4 27.8 %dynamic-update-slice.4 = f32[4715520]{0:T(1024)} dynamic-update-slice(f32[4715520]{0:T(1024)} %get-tuple-element.108, f32[785920]{0:T(1024)} %dynamic-slice_reduce_fusion.4, u32[]{:T(128)S(6)} %add.194) | dynamic-update-slice | bytes 6287364
  304.7 37.0 %dynamic-slice_reduce_fusion.4 = f32[785920]{0:T(1024)} fusion(f32[]{:T(128)} %broadcast.187, f32[1,6,785920]{2,1,0:T(8,128)} %get-tuple-element.115, u32[]{:T(128)S(6)} %multiply.52, u32[]{:T(128)S(6)} %multiply.53), kind=kLoop, calls=%fused_computation.133.clone.1 | loop fusion | bytes 6287372
  341.7 27.8 %dynamic-update-slice.4 = f32[4715520]{0:T(1024)} dynamic-update-slice(f32[4715520]{0:T(1024)} %get-tuple-element.108, f32[785920]{0:T(1024)} %dynamic-slice_reduce_fusion.4, u32[]{:T(128)S(6)} %add.194) | dynamic-update-slice | bytes 6287364
  370.0 37.0 %dynamic-slice_reduce_fusion.4 = f32[785920]{0:T(1024)} fusion(f32[]{:T(128)} %broadcast.187, f32[1,6,785920]{2,1,0:T(8,128)} %get-tuple-element.115, u32[]{:T(128)S(6)} %multiply.52, u32[]{:T(128)S(6)} %multiply.53), kind=kLoop, calls=%fused_computation.133.clone.1 | loop fusion | bytes 6287372
  407.1 27.8 %dynamic-update-slice.4 = f32[4715520]{0:T(1024)} dynamic-update-slice(f32[4715520]{0:T(1024)} %get-tuple-element.108, f32[785920]{0:T(1024)} %dynamic-slice_reduce_fusion.4, u32[]{:T(128)S(6)} %add.194) | dynamic-update-slice | bytes 6287364
  435.4 37.0 %dynamic-slice_reduce_fusion.4 = f32[785920]{0:T(1024)} fusion(f32[]{:T(128)} %broadcast.187, f32[1,6,785920]{2,1,0:T(8,128)} %get-tuple-element.115, u32[]{:T(128)S(6)} %multiply.52, u32[]{:T(128)S(6)} %multiply.53), kind=kLoop, calls=%fused_computation.133.clone.1 | loop fusion | bytes 6287372
  472.4 27.4 %dynamic-update-slice.4 = f32[4715520]{0:T(1024)} dynamic-update-slice(f32[4715520]{0:T(1024)} %get-tuple-element.108, f32[785920]{0:T(1024)} %dynamic-slice_reduce_fusion.4, u32[]{:T(128)S(6)} %add.194) | dynamic-update-slice | bytes 6287364
  499.8 29.5 %reshape.159 = f32[6,512,1535]{2,1,0:T(8,128)} reshape(f32[4715520]{0:T(1024)} %get-tuple-element.16) | data formatting | bytes 37724160 | tf_op jit(solution)/shard_map/reshape | solution.py:69
  546.4 19.7 %all-reduce.11.cloned.1.call-done = f32[512,768]{1,0:T(8,128)} async-done(((f32[512,768]{1,0:T(8,128)}), f32[512,768]{1,0:T(8,128)}) %all-reduce.11.cloned.1.call-update) | async-done | bytes 1572880 | tf_op jit(solution)/shard_map/psum | solution.py:135
  585.1 13.6 all-to-all-done
  636.6 20.2 %all-reduce.14 = (bf16[1024,768]{1,0:T(8,128)(2,1)}, bf16[1024,768]{1,0:T(8,128)(2,1)}) all-reduce(f32[1024,768]{1,0:T(8,128)S(1)} %copy-done.17, f32[1024,768]{1,0:T(8,128)} %fusion.19), channel_id=1, replica_groups=mesh['dp'=8,'row'=2,'col'=2] {'col'}, use_global_device_ids=true, to_apply=%region_12.13 | all-reduce | flops 1572864 | bytes 9437184 | tf_op jit(solution)/shard_map/psum | solution.py:183
  656.7 23.7 %all_to_all.20 = bf16[2,512,768]{2,1,0:T(8,128)(2,1)S(1)} all-to-all(bf16[2,512,768]{2,1,0:T(8,128)(2,1)} %bitcast.138), channel_id=1, replica_groups=mesh['dp'=8,'row'=2,'col'=2] {'row'}, dimensions={0} | all-to-all | bytes 3145728 | tf_op jit(solution)/shard_map/all_to_all | solution.py:192
  687.2 16.2 %all-to-all-done.1 = bf16[2,512,768]{2,1,0:T(8,128)(2,1)S(1)} async-done(((bf16[2,512,768]{2,1,0:T(8,128)(2,1)}), bf16[2,512,768]{2,1,0:T(8,128)(2,1)S(1)}, u32[]{:S(2)}, u32[]{:S(2)}) %all-to-all-start.1) | async-done | bytes 1572896 | tf_op jit(solution)/shard_map/all_to_all | solution.py:185
  714.6 10.5 multiply_reduce_fusion
  755.1 16.8 %reduce-scatter.14.cloned.1.call-done = bf16[512,384]{0,1:T(8,128)(2,1)} async-done(((bf16[1024,384]{0,1:T(8,128)(2,1)}), bf16[512,384]{0,1:T(8,128)(2,1)}) %reduce-scatter.14.cloned.1.call-update) | async-done | bytes 393232 | tf_op jit(solution)/shard_map/reduce_scatter | solution.py:242
  803.0 12.9 copy.36
  817.9 12.5 fusion.85
  832.2 341.3 %while.3 = (u32[]{:T(128)}, f32[1,6,786944]{2,1,0:T(8,128)}, f32[4721664]{0:T(1024)}, u32[]{}, f32[]{:T(128)}, /*index=5*/u32[]{}, u32[]{}, u32[]{}) while((u32[]{:T(128)}, f32[1,6,786944]{2,1,0:T(8,128)}, f32[4721664]{0:T(1024)}, u32[]{}, f32[]{:T(128)}, /*index=5*/u32[]{}, u32[]{}, u32[]{}) %tuple.43), condition=%wide.cond.1, body=%wide.body.1.sunk | while | flops 9 | bytes 12591305
  832.8 30.0 %dynamic-slice_reduce_fusion.5 = f32[786944]{0:T(1024)S(1)} fusion(f32[]{:T(128)} %broadcast.188, f32[1,6,786944]{2,1,0:T(8,128)} %get-tuple-element.139, u32[]{:T(128)S(6)} %multiply.56, u32[]{:T(128)S(6)} %multiply.57), kind=kLoop, calls=%fused_computation.134.clone.1 | loop fusion | bytes 6295564
  862.7 26.4 %dynamic-update-slice.5 = f32[4721664]{0:T(1024)} dynamic-update-slice(f32[4721664]{0:T(1024)} %get-tuple-element.132, f32[786944]{0:T(1024)S(1)} %dynamic-slice_reduce_fusion.5, u32[]{:T(128)S(6)} %add.196) | dynamic-update-slice | bytes 6295556
  889.6 30.0 %dynamic-slice_reduce_fusion.5 = f32[786944]{0:T(1024)S(1)} fusion(f32[]{:T(128)} %broadcast.188, f32[1,6,786944]{2,1,0:T(8,128)} %get-tuple-element.139, u32[]{:T(128)S(6)} %multiply.56, u32[]{:T(128)S(6)} %multiply.57), kind=kLoop, calls=%fused_computation.134.clone.1 | loop fusion | bytes 6295564
  919.6 26.4 %dynamic-update-slice.5 = f32[4721664]{0:T(1024)} dynamic-update-slice(f32[4721664]{0:T(1024)} %get-tuple-element.132, f32[786944]{0:T(1024)S(1)} %dynamic-slice_reduce_fusion.5, u32[]{:T(128)S(6)} %add.196) | dynamic-update-slice | bytes 6295556
  946.5 30.0 %dynamic-slice_reduce_fusion.5 = f32[786944]{0:T(1024)S(1)} fusion(f32[]{:T(128)} %broadcast.188, f32[1,6,786944]{2,1,0:T(8,128)} %get-tuple-element.139, u32[]{:T(128)S(6)} %multiply.56, u32[]{:T(128)S(6)} %multiply.57), kind=kLoop, calls=%fused_computation.134.clone.1 | loop fusion | bytes 6295564
  976.4 26.5 %dynamic-update-slice.5 = f32[4721664]{0:T(1024)} dynamic-update-slice(f32[4721664]{0:T(1024)} %get-tuple-element.132, f32[786944]{0:T(1024)S(1)} %dynamic-slice_reduce_fusion.5, u32[]{:T(128)S(6)} %add.196) | dynamic-update-slice | bytes 6295556
  1003.4 30.0 %dynamic-slice_reduce_fusion.5 = f32[786944]{0:T(1024)S(1)} fusion(f32[]{:T(128)} %broadcast.188, f32[1,6,786944]{2,1,0:T(8,128)} %get-tuple-element.139, u32[]{:T(128)S(6)} %multiply.56, u32[]{:T(128)S(6)} %multiply.57), kind=kLoop, calls=%fused_computation.134.clone.1 | loop fusion | bytes 6295564
  1033.3 26.5 %dynamic-update-slice.5 = f32[4721664]{0:T(1024)} dynamic-update-slice(f32[4721664]{0:T(1024)} %get-tuple-element.132, f32[786944]{0:T(1024)S(1)} %dynamic-slice_reduce_fusion.5, u32[]{:T(128)S(6)} %add.196) | dynamic-update-slice | bytes 6295556
  1060.3 30.0 %dynamic-slice_reduce_fusion.5 = f32[786944]{0:T(1024)S(1)} fusion(f32[]{:T(128)} %broadcast.188, f32[1,6,786944]{2,1,0:T(8,128)} %get-tuple-element.139, u32[]{:T(128)S(6)} %multiply.56, u32[]{:T(128)S(6)} %multiply.57), kind=kLoop, calls=%fused_computation.134.clone.1 | loop fusion | bytes 6295564
  1090.3 26.4 %dynamic-update-slice.5 = f32[4721664]{0:T(1024)} dynamic-update-slice(f32[4721664]{0:T(1024)} %get-tuple-element.132, f32[786944]{0:T(1024)S(1)} %dynamic-slice_reduce_fusion.5, u32[]{:T(128)S(6)} %add.196) | dynamic-update-slice | bytes 6295556
  1117.2 30.0 %dynamic-slice_reduce_fusion.5 = f32[786944]{0:T(1024)S(1)} fusion(f32[]{:T(128)} %broadcast.188, f32[1,6,786944]{2,1,0:T(8,128)} %get-tuple-element.139, u32[]{:T(128)S(6)} %multiply.56, u32[]{:T(128)S(6)} %multiply.57), kind=kLoop, calls=%fused_computation.134.clone.1 | loop fusion | bytes 6295564
  1147.2 26.3 %dynamic-update-slice.5 = f32[4721664]{0:T(1024)} dynamic-update-slice(f32[4721664]{0:T(1024)} %get-tuple-element.132, f32[786944]{0:T(1024)S(1)} %dynamic-slice_reduce_fusion.5, u32[]{:T(128)S(6)} %add.196) | dynamic-update-slice | bytes 6295556
  1173.5 31.3 %reshape.172 = f32[6,512,1537]{2,1,0:T(8,128)} reshape(f32[4721664]{0:T(1024)} %get-tuple-element.21) | data formatting | bytes 37773312 | tf_op jit(solution)/shard_map/convert_element_type | solution.py:56
  1216.4 76.1 %all-reduce.5 = (f32[768]{0:T(1024)S(1)}, f32[32,6]{0,1:T(8,128)}, f32[768]{0:T(1024)S(1)}) all-reduce(f32[768]{0:T(1024)S(1)} %get-tuple-element.24, f32[32,6]{0,1:T(8,128)S(1)} %fusion.61, f32[768]{0:T(1024)S(1)} %copy-done.41), channel_id=4, replica_groups=mesh['dp'=8,'row'=2,'col'=2] {'dp','row'}, use_global_device_ids=true, to_apply=%region_23.24.clone | all-reduce | flops 1728 | bytes 13824
  1300.7 22.3 %reduce-scatter.16.cloned.1.call-done = f32[48,384]{1,0:T(8,128)} async-done(((f32[768,384]{1,0:T(8,128)}), f32[48,384]{1,0:T(8,128)}) %reduce-scatter.16.cloned.1.call-update) | async-done | bytes 73744 | tf_op jit(solution)/shard_map/reduce_scatter | solution.py:273
  1323.0 128.5 %reduce-scatter.20.cloned.1.call-done = f32[48,384]{1,0:T(8,128)} async-done(((f32[768,384]{1,0:T(8,128)}), f32[48,384]{1,0:T(8,128)}) %reduce-scatter.20.cloned.1.call-update) | async-done | bytes 73744 | tf_op jit(solution)/shard_map/reduce_scatter | solution.py:275
  1451.5 128.6 %reduce-scatter.18.cloned.1.call-done = f32[48,384]{1,0:T(8,128)} async-done(((f32[768,384]{1,0:T(8,128)}), f32[48,384]{1,0:T(8,128)}) %reduce-scatter.18.cloned.1.call-update) | async-done | bytes 73744 | tf_op jit(solution)/shard_map/reduce_scatter | solution.py:274
  (226 shorter events, 207.9 us)
Async XLA Ops:
  7.2 603.6 %copy-start = (bf16[1,768,1536]{2,1,0:T(8,128)(2,1)S(1)}, bf16[1,768,1536]{2,1,0:T(8,128)(2,1)}, u32[]{:S(2)}) copy-start(bf16[1,768,1536]{2,1,0:T(8,128)(2,1)} %param.27) | copy-start | bytes 7077892
  7.2 22.9 %copy-start.5 = (bf16[512,768]{1,0:T(8,128)(2,1)S(1)}, bf16[512,768]{1,0:T(8,128)(2,1)}, u32[]{:S(2)}) copy-start(bf16[512,768]{1,0:T(8,128)(2,1)} %param.14) | copy-start | bytes 2359300
  7.2 558.8 %all-reduce.11.cloned.1.call-start = ((), (), s32[]{:S(2)}) async-start(), calls=%async_computation.13 | async-start | bytes 3145728 | tf_op jit(solution)/shard_map/psum | solution.py:135
  9.4 42.0 %copy-start.34 = (f32[512]{0:T(512)}, f32[512]{0:T(512)S(1)}, u32[]{:S(2)}) copy-start(f32[512]{0:T(512)S(1)} %get-tuple-element.50) | copy-start | bytes 6148
  10.1 41.3 %copy-start.29 = (f32[768]{0:T(1024)}, f32[768]{0:T(1024)S(1)}, u32[]{:S(2)}) copy-start(f32[768]{0:T(1024)S(1)} %convert_element_type.146) | copy-start | bytes 9220
  21.0 10.3 copy-start.20
  30.7 498.6 %copy-start.22 = (bf16[512,384]{0,1:T(8,128)(2,1)}, bf16[512,384]{0,1:T(8,128)(2,1)S(1)}, u32[]{:S(2)}) copy-start(bf16[512,384]{0,1:T(8,128)(2,1)S(1)} %convolution_convert_fusion.5) | copy-start | bytes 1179652
  52.9 19.4 %copy-start.38 = (s32[2047]{0:T(1024)S(1)}, s32[2047]{0:T(1024)}, u32[]{:S(2)}) copy-start(s32[2047]{0:T(1024)} %param.23) | copy-start | bytes 24568
  52.9 19.4 %copy-start.45 = (bf16[32,12]{0,1:T(8,128)(2,1)S(1)}, bf16[32,12]{0,1:T(8,128)(2,1)}, u32[]{:S(2)}) copy-start(bf16[32,12]{0,1:T(8,128)(2,1)} %param.22) | copy-start | bytes 2308
  536.8 5.8 copy-start.2
  539.5 4.0 copy-start.13
  545.2 165.0 %copy-start.28 = (f32[768]{0:T(1024)}, f32[768]{0:T(1024)S(1)}, u32[]{:S(2)}) copy-start(f32[768]{0:T(1024)S(1)} %convert_element_type.155) | copy-start | bytes 9220
  568.8 141.4 %copy-start.36 = (f32[512]{0:T(512)}, f32[512]{0:T(512)S(1)}, u32[]{:S(2)}) copy-start(f32[512]{0:T(512)S(1)} %get-tuple-element.52) | copy-start | bytes 6148
  573.5 5.2 copy-start.42
  573.5 7.7 copy-start.9
  573.5 25.2 %all-to-all-start = ((bf16[2,512,768]{2,1,0:T(8,128)(2,1)}), bf16[2,512,768]{2,1,0:T(8,128)(2,1)}, u32[]{:S(2)}, u32[]{:S(2)}) async-start(bf16[2,512,768]{2,1,0:T(8,128)(2,1)} %bitcast.123), calls=%async_computation | async-start | bytes 3145728 | tf_op jit(solution)/shard_map/all_to_all | solution.py:167
  581.2 124.6 %copy-start.37 = (f32[512,2]{0,1:T(2,128)}, f32[512,2]{0,1:T(2,128)S(1)}, u32[]{:S(2)}) copy-start(f32[512,2]{0,1:T(2,128)S(1)} %get-tuple-element.44) | copy-start | bytes 12292
  598.7 23.9 %all-to-all-start.2 = ((bf16[2,512,768]{2,1,0:T(8,128)(2,1)}), bf16[2,512,768]{2,1,0:T(8,128)(2,1)}, u32[]{:S(2)}, u32[]{:S(2)}) async-start(bf16[2,512,768]{2,1,0:T(8,128)(2,1)} %bitcast.124), calls=%async_computation.2 | async-start | bytes 3145728 | tf_op jit(solution)/shard_map/all_to_all | solution.py:168
  622.6 9.7 copy-start.46
  632.3 4.3 copy-start.17
  680.4 4.1 copy-start.32
  680.4 23.0 %all-to-all-start.1 = ((bf16[2,512,768]{2,1,0:T(8,128)(2,1)}), bf16[2,512,768]{2,1,0:T(8,128)(2,1)S(1)}, u32[]{:S(2)}, u32[]{:S(2)}) async-start(bf16[2,512,768]{2,1,0:T(8,128)(2,1)} %bitcast.137), calls=%async_computation.1 | async-start | bytes 3145728 | tf_op jit(solution)/shard_map/all_to_all | solution.py:185
  684.2 67.9 %reduce-scatter.12.cloned.1.call-start = ((), (), s32[]{:S(2)}) async-start(), calls=%async_computation.14 | async-start | bytes 1179648 | tf_op jit(solution)/shard_map/reduce_scatter | solution.py:239
  705.5 4.7 copy-start.12
  705.8 4.4 copy-start.11
  705.8 7.1 copy-start.40
  713.0 76.5 %copy-start.8 = (f32[512,768]{1,0:T(8,128)}, f32[512,768]{1,0:T(8,128)S(1)}, u32[]{:S(2)}) copy-start(f32[512,768]{1,0:T(8,128)S(1)} %get-tuple-element.47) | copy-start | bytes 4718596
  713.5 11.6 slice-start
  714.6 10.5 slice-start.1
  714.6 10.5 slice-start.2
  725.2 6.3 copy-start.23
  734.3 37.6 %reduce-scatter.14.cloned.1.call-start = ((), (), s32[]{:S(2)}) async-start(), calls=%async_computation.15 | async-start | bytes 1179648 | tf_op jit(solution)/shard_map/reduce_scatter | solution.py:242
  741.2 471.9 %reduce-scatter.28.cloned.1.call-start = ((), (), s32[]{:S(2)}) async-start(), calls=%async_computation.23 | async-start | bytes 417792
  745.6 5.1 copy-start.21
  751.3 463.2 %all-reduce.13.cloned.1.call-start = ((), (), s32[]{:S(2)}) async-start(), calls=%async_computation.16 | async-start | bytes 1572864 | tf_op jit(solution)/shard_map/psum | solution.py:260
  775.1 521.9 %reduce-scatter.26.cloned.1.call-start = ((), (), s32[]{:S(2)}) async-start(), calls=%async_computation.22 | async-start | bytes 2654208 | tf_op jit(solution)/shard_map/reduce_scatter | solution.py:207
  782.8 516.1 %reduce-scatter.24.cloned.1.call-start = ((), (), s32[]{:S(2)}) async-start(), calls=%async_computation.21 | async-start | bytes 2654208 | tf_op jit(solution)/shard_map/reduce_scatter | solution.py:204
  789.4 511.3 %reduce-scatter.22.cloned.1.call-start = ((), (), s32[]{:S(2)}) async-start(), calls=%async_computation.20 | async-start | bytes 1253376 | tf_op jit(solution)/shard_map/reduce_scatter | solution.py:276
  791.9 3.7 copy-start.39
  792.0 531.1 %reduce-scatter.16.cloned.1.call-start = ((), (), s32[]{:S(2)}) async-start(), calls=%async_computation.17 | async-start | bytes 1253376 | tf_op jit(solution)/shard_map/reduce_scatter | solution.py:273
  794.3 657.2 %reduce-scatter.20.cloned.1.call-start = ((), (), s32[]{:S(2)}) async-start(), calls=%async_computation.19 | async-start | bytes 1253376 | tf_op jit(solution)/shard_map/reduce_scatter | solution.py:275
  803.0 13.0 copy-start.27
  817.8 762.3 %reduce-scatter.18.cloned.1.call-start = ((), (), s32[]{:S(2)}) async-start(), calls=%async_computation.18 | async-start | bytes 1253376 | tf_op jit(solution)/shard_map/reduce_scatter | solution.py:274
  817.9 12.6 copy-start.26
  1204.8 9.7 copy-start.7
  1204.8 11.6 copy-start.41
  1204.9 88.8 %copy-start.43 = (f32[512]{0:T(512)S(1)}, f32[512]{0:T(512)}, u32[]{:S(2)}) copy-start(f32[512]{0:T(512)} %get-tuple-element.49) | copy-start | bytes 6148
  1293.7 286.5 %copy-start.1 = (bf16[1,768,1536]{2,1,0:T(8,128)(2,1)S(1)}, bf16[1,768,1536]{2,1,0:T(8,128)(2,1)}, u32[]{:S(2)}) copy-start(bf16[1,768,1536]{2,1,0:T(8,128)(2,1)} %param.27) | copy-start | bytes 7077892
  (19 other events, 41.3 us)
Sparse Core Ops, SparseCore 0:
  545.3 20.6 all-reduce.10
  734.5 17.6 reduce-scatter.11
  754.4 17.4 reduce-scatter.13
  777.1 121.6 reduce-scatter.27
  901.0 18.2 all-reduce.12
  923.1 70.4 reduce-scatter.25
  997.4 68.0 reduce-scatter.23
  1071.5 122.6 reduce-scatter.21
  1200.3 122.7 reduce-scatter.15
  1328.9 122.5 reduce-scatter.19
  1457.6 122.5 reduce-scatter.17
where the time goes:
time: 1610 us; the launch traced here: 1590 us
  local copies, waits for them, and re-layouts  872 us (54%)
  waiting for transfers between devices  353 us (22%)
  blocking collectives  175 us (11%)
  matrix products  99.8 us (6%)
  other arithmetic  56.6 us (4%)
    unnamed x151, local copies, waits for them, and re-layouts  802 us
    reduce_scatter x1, waiting for transfers between devices, local(): lax.psum_scatter(grad_w_key, ('dp', 'row'), scatter_dimension=0, tiled=True)  129 us
    reduce_scatter x1, waiting for transfers between devices, local(): lax.psum_scatter(grad_w_value, ('dp', 'row'), scatter_dimension=0, tiled=...  128 us
    unnamed x1, blocking collectives  76.1 us
  transfers between devices with their start and end apart: 14, of which 9 were waited for; matrix products, arithmetic and copies ran while one was open for 31% of the time, Pallas kernels for 0%

commit v1 on v0

--- a/solution.py
+++ b/solution.py
@@ -1,6 +1,10 @@
+import functools
+
 import jax
 import jax.numpy as jnp
 from jax import lax
+from jax.experimental import pallas as pl
+from jax.experimental.pallas import tpu as pltpu
 from jax.sharding import PartitionSpec as P
 
 H = 12
@@ -294,6 +298,752 @@
     )
 
 
+VMEM = pltpu.VMEM
+SMEM = pltpu.SMEM
+
+
+def dot_nn(a, b):
+    return lax.dot_general(a, b, (((1,), (0,)), ((), ())), preferred_element_type=WIDE)
+
+
+def dot_nt(a, b):
+    return lax.dot_general(a, b, (((1,), (1,)), ((), ())), preferred_element_type=WIDE)
+
+
+def dot_tn(a, b):
+    return lax.dot_general(a, b, (((0,), (0,)), ((), ())), preferred_element_type=WIDE)
+
+
+def full_spec(shape):
+    return pl.BlockSpec(shape, lambda *_: (0,) * len(shape))
+
+
+def smem_spec():
+    return pl.BlockSpec(memory_space=SMEM)
+
+
+def params(megabytes=48):
+    return pltpu.CompilerParams(vmem_limit_bytes=megabytes * 1024 * 1024)
+
+
+def cost(flops, moved):
+    return pl.CostEstimate(flops=int(flops), bytes_accessed=int(moved), transcendentals=0)
+
+
+def shape_of(shape, dtype):
+    return jax.ShapeDtypeStruct(shape, dtype)
+
+
+def project_kernel(place, tok, gain, w_own, w_oth, normed, q, k, v, w_all):
+    half = w_own.shape[0]
+    row = place[0]
+
+    @pl.when(jnp.logical_and(pl.program_id(0) == 0, row == 0))
+    def _():
+        w_all[:half] = w_own[...]
+        w_all[half:] = w_oth[...]
+
+    @pl.when(jnp.logical_and(pl.program_id(0) == 0, row == 1))
+    def _():
+        w_all[:half] = w_oth[...]
+        w_all[half:] = w_own[...]
+
+    rows = tok[...].astype(WIDE)
+    inverse = lax.rsqrt(jnp.mean(rows * rows, axis=-1, keepdims=True) + EPS)
+    low = (rows * inverse * gain[...].astype(WIDE)).astype(NARROW)
+    normed[...] = low
+    out = dot_nn(low, w_all[...])
+    heads, _, size = q.shape
+    wide = heads * size
+    for h in range(heads):
+        q[h] = (out[:, h * size : (h + 1) * size] * SCALE).astype(NARROW)
+        k[h] = out[:, wide + h * size : wide + (h + 1) * size].astype(NARROW)
+        v[h] = out[:, 2 * wide + h * size : 2 * wide + (h + 1) * size].astype(NARROW)
+
+
+def project(place, tok_all, gain, w_own, w_oth, heads, size, block):
+    seq, width = tok_all.shape
+    cols = w_own.shape[1]
+    head_spec = pl.BlockSpec((heads, block, size), lambda i: (0, i, 0))
+    row_spec = pl.BlockSpec((block, width), lambda i: (i, 0))
+    head_shape = shape_of((heads, seq, size), NARROW)
+    return pl.pallas_call(
+        project_kernel,
+        grid=(seq // block,),
+        in_specs=[smem_spec(), row_spec, full_spec(gain.shape), full_spec(w_own.shape), full_spec(w_oth.shape)],
+        out_specs=[row_spec, head_spec, head_spec, head_spec, full_spec((width, cols))],
+        out_shape=[shape_of((seq, width), NARROW)] + [head_shape] * 3 + [shape_of((width, cols), NARROW)],
+        compiler_params=params(),
+        cost_estimate=cost(2 * seq * width * cols, 4 * seq * width * 2),
+        name="project",
+    )(place, tok_all, gain, w_own, w_oth)
+
+
+TILE = 128
+
+
+def bias_lanes(row, block_index, blocks):
+    half = blocks // 2
+    query = lax.rem(block_index + half * row, blocks)
+    own = half * row - query + blocks
+    other = half * (1 - row) - query + blocks
+    return pl.multiple_of(own * TILE, TILE), pl.multiple_of(other * TILE, TILE)
+
+
+def attend_kernel(first, place, bucket, table, q, k, v, att, p, skew):
+    heads, block, size = q.shape
+    seq = k.shape[1]
+    half = seq // 2
+    row = place[0]
+    step = pl.program_id(0)
+
+    @pl.when(step == 0)
+    def _():
+        n = bucket.shape[1]
+        hot = (bucket[...] == lax.broadcasted_iota(jnp.int32, (NBUCKET, n), 0)).astype(WIDE)
+        for h in range(heads):
+            line = jnp.sum(hot * table[:, h : h + 1], axis=0, keepdims=True)
+            skew[h] = pltpu.roll(jnp.broadcast_to(line, (TILE, n)), 0, 1, stride=1, stride_axis=0)
+
+    for h in range(heads):
+        raw = dot_nt(q[h], k[h])
+        parts = []
+        for sub in range(block // TILE):
+            own, other = bias_lanes(row, first + step * (block // TILE) + sub, seq // TILE)
+            bias = jnp.concatenate([skew[h, :, pl.ds(own, half)], skew[h, :, pl.ds(other, half)]], axis=1)
+            scores = raw[sub * TILE : (sub + 1) * TILE] + bias
+            raised = jnp.exp(scores - jnp.max(scores, axis=1, keepdims=True))
+            share = raised * (1.0 / jnp.sum(raised, axis=1, keepdims=True))
+            parts.append(share.astype(NARROW))
+        shares = jnp.concatenate(parts, axis=0)
+        p[h] = shares
+        att[:, h * size : (h + 1) * size] = dot_nn(shares, v[h]).astype(NARROW)
+
+
+def attend(place, bucket, table, q, k, v, block, begin, rows):
+    heads, seq, size = q.shape
+    start = begin // block
+    return pl.pallas_call(
+        functools.partial(attend_kernel, begin // TILE),
+        grid=(rows // block,),
+        in_specs=[
+            smem_spec(),
+            full_spec(bucket.shape),
+            full_spec(table.shape),
+            pl.BlockSpec((heads, block, size), lambda i: (0, i + start, 0)),
+            full_spec(k.shape),
+            full_spec(v.shape),
+        ],
+        out_specs=[
+            pl.BlockSpec((block, heads * size), lambda i: (i, 0)),
+            pl.BlockSpec((heads, block, seq), lambda i: (0, i, 0)),
+        ],
+        out_shape=[shape_of((rows, heads * size), NARROW), shape_of((heads, rows, seq), NARROW)],
+        scratch_shapes=[VMEM((heads, TILE, bucket.shape[1]), WIDE)],
+        compiler_params=params(),
+        cost_estimate=cost(8 * heads * rows * seq * 128, heads * rows * seq * 4),
+        name="attend",
+    )(place, bucket, table, q, k, v)
+
+
+def attend_back_kernel(first, last, place, bucket, q, k, v, p, g, *refs):
+    if first == 0:
+        keep_in = None
+    else:
+        keep_in, refs = refs[:3], refs[3:]
+    if last:
+        out, table, key_sum, value_sum, diag = refs
+        query_out = None
+    else:
+        query_out, key_sum, value_sum, diag = refs
+        out = None
+    heads, block, size = q.shape
+    seq = k.shape[1]
+    half = seq // 2
+    row = place[0]
+    step = pl.program_id(0)
+
+    @pl.when(step == 0)
+    def _():
+        if keep_in is None:
+            key_sum[...] = jnp.zeros_like(key_sum)
+            value_sum[...] = jnp.zeros_like(value_sum)
+            diag[...] = jnp.zeros_like(diag)
+        else:
+            key_sum[...] = keep_in[0][...]
+            value_sum[...] = keep_in[1][...]
+            diag[...] = keep_in[2][...]
+
+    wide = heads * size
+    for h in range(heads):
+        grad = g[:, h * size : (h + 1) * size]
+        share_low = p[h]
+        share = share_low.astype(WIDE)
+        grad_share = dot_nt(grad, v[h])
+        delta = jnp.sum(share * grad_share, axis=1, keepdims=True)
+        grad_score = share * (grad_share - delta)
+        for sub in range(block // TILE):
+            own, other = bias_lanes(row, first + step * (block // TILE) + sub, seq // TILE)
+            piece = grad_score[sub * TILE : (sub + 1) * TILE]
+            diag[h, :, pl.ds(own, half)] += piece[:, :half]
+            diag[h, :, pl.ds(other, half)] += piece[:, half:]
+        low = grad_score.astype(NARROW)
+        grad_query = (SCALE * dot_nn(low, k[h])).astype(NARROW)
+        if last:
+            out[pl.ds(pl.multiple_of(first * TILE + step * block, block), block), h * size : (h + 1) * size] = grad_query
+        else:
+            query_out[:, h * size : (h + 1) * size] = grad_query
+        key_sum[h] += dot_tn(q[h], low)
+        value_sum[h] += dot_tn(grad, share_low)
+
+    if last:
+        lanes = diag.shape[2]
+
+        @pl.when(step == pl.num_programs(0) - 1)
+        def _():
+            hot = (bucket[...] == lax.broadcasted_iota(jnp.int32, (NBUCKET, lanes), 0)).astype(WIDE)
+            lane = lax.broadcasted_iota(jnp.int32, table.shape, 1)
+            total = jnp.zeros(table.shape, WIDE)
+            for h in range(heads):
+                lo = h * size
+                out[:, wide + lo : wide + lo + size] = key_sum[h].T.astype(NARROW)
+                out[:, 2 * wide + lo : 2 * wide + lo + size] = value_sum[h].T.astype(NARROW)
+                sums = diag[h]
+                height = TILE // 2
+                while height >= 8:
+                    sums = sums[:height] + pltpu.roll(sums[height:], lanes - height, 1)
+                    height //= 2
+                where = lax.broadcasted_iota(jnp.int32, sums.shape, 0)
+                for bit in (4, 2, 1):
+                    sums = jnp.where((where & bit) != 0, pltpu.roll(sums, lanes - bit, 1), sums)
+                line = jnp.sum(sums, axis=0, keepdims=True)
+                total = total + jnp.where(lane == h, jnp.sum(hot * line, axis=1, keepdims=True), 0.0)
+            table[...] = total
+
+
+def attend_back(place, bucket, q, k, v, p, g, block, begin, keep):
+    heads, seq, size = q.shape
+    rows = g.shape[0]
+    start = begin // block
+    last = keep is not None
+    lanes = bucket.shape[1]
+    sum_shape = (heads, size, seq)
+    diag_shape = (heads, TILE, lanes)
+    wide = heads * size
+    in_specs = [
+        smem_spec(),
+        full_spec(bucket.shape),
+        pl.BlockSpec((heads, block, size), lambda i: (0, i + start, 0)),
+        full_spec(k.shape),
+        full_spec(v.shape),
+        pl.BlockSpec((heads, block, seq), lambda i: (0, i, 0)),
+        pl.BlockSpec((block, wide), lambda i: (i, 0)),
+    ]
+    args = [place, bucket, q, k, v, p, g]
+    sums = [shape_of(sum_shape, WIDE), shape_of(sum_shape, WIDE), shape_of(diag_shape, WIDE)]
+    if last:
+        in_specs += [full_spec(s.shape) for s in sums]
+        args += list(keep[1:])
+        in_specs += [full_spec(keep[0].shape)]
+        args += [keep[0]]
+        out_specs = [full_spec((seq, 3 * wide)), full_spec((NBUCKET, 128))]
+        out_shape = [shape_of((seq, 3 * wide), NARROW), shape_of((NBUCKET, 128), WIDE)]
+        scratch = [VMEM(s.shape, WIDE) for s in sums]
+
+        def kernel(*refs):
+            earlier = refs[10]
+            out = refs[11]
+
+            @pl.when(pl.program_id(0) == 0)
+            def _():
+                out[: earlier.shape[0], :wide] = earlier[...]
+
+            attend_back_kernel(begin // TILE, True, *refs[:10], *refs[11:])
+
+    else:
+        out_specs = [pl.BlockSpec((block, wide), lambda i: (i, 0))] + [full_spec(s.shape) for s in sums]
+        out_shape = [shape_of((rows, wide), NARROW)] + sums
+        scratch = []
+        kernel = functools.partial(attend_back_kernel, begin // TILE, False)
+    return pl.pallas_call(
+        kernel,
+        grid=(rows // block,),
+        in_specs=in_specs,
+        out_specs=out_specs,
+        out_shape=out_shape,
+        scratch_shapes=scratch,
+        compiler_params=params(),
+        cost_estimate=cost(14 * heads * rows * seq * 128, heads * rows * seq * 4),
+        name="attend_back",
+    )(*args)
+
+
+def gate_values(hn, route, router):
+    count = router.shape[0]
+    logits = [jnp.sum(hn * router[e : e + 1], axis=1, keepdims=True) for e in range(count)]
+    top = functools.reduce(jnp.maximum, logits)
+    raised = [jnp.exp(x - top) for x in logits]
+    total = functools.reduce(jnp.add, raised)
+    probs = [x / total for x in raised]
+    hots = [(route == e).astype(WIDE) for e in range(count)]
+    gate = functools.reduce(jnp.add, [p * o for p, o in zip(probs, hots)])
+    return probs, hots, gate
+
+
+def hidden_kernel(place, a_mine, a_row, a_col, a_diag, w_mine, w_other, tok, gain, router, route, grad, hidden, att, rows, grads, pack):
+    row = place[0]
+    step = pl.program_id(0)
+    size = a_mine.shape[1]
+
+    @pl.when(row == 0)
+    def _():
+        pack[0, :, :size] = a_mine[...]
+        pack[0, :, size:] = a_row[...]
+        pack[1, :, :size] = a_col[...]
+        pack[1, :, size:] = a_diag[...]
+
+    @pl.when(row == 1)
+    def _():
+        pack[0, :, size:] = a_mine[...]
+        pack[0, :, :size] = a_row[...]
+        pack[1, :, size:] = a_col[...]
+        pack[1, :, :size] = a_diag[...]
+
+    branch = dot_nt(pack[0], w_mine[...]) + dot_nt(pack[1], w_other[...])
+    wide = tok[...].astype(WIDE) + branch
+
+    @pl.when(step < 2)
+    def _():
+        hidden[...] = wide
+        att[...] = pack[0]
+
+    inverse = lax.rsqrt(jnp.mean(wide * wide, axis=-1, keepdims=True) + EPS)
+    hn = wide * inverse * gain[...].astype(WIDE)
+    kind = route[...]
+    _, hots, gate = gate_values(hn, kind, router)
+    chosen = jnp.where(kind == row, 1.0, 0.0)
+    rows[...] = (hn * chosen).astype(NARROW)
+    grads[...] = (grad[...].astype(WIDE) * (gate * chosen)).astype(NARROW)
+
+
+def hidden_rows(place, pieces, w_mine, w_other, tok_all, gain, router, route_all, grad_all):
+    seq, width = tok_all.shape
+    block = seq // 4
+    size = pieces[0].shape[1]
+    half = w_mine.shape[1]
+    turned = pl.BlockSpec((block, size), lambda i: (lax.rem(i + 2, 4), 0))
+    plain = pl.BlockSpec((block, size), lambda i: (i, 0))
+    wide_spec = pl.BlockSpec((block, width), lambda i: (i, 0))
+    own_spec = pl.BlockSpec((block, width), lambda i: (jnp.minimum(i, 1), 0))
+    mixed = pl.BlockSpec((block, width), lambda i: (lax.rem(i, 2) * 2 + lax.div(i, 2), 0))
+    return pl.pallas_call(
+        hidden_kernel,
+        grid=(4,),
+        in_specs=[
+            smem_spec(),
+            plain,
+            turned,
+            plain,
+            turned,
+            full_spec(w_mine.shape),
+            full_spec(w_other.shape),
+            wide_spec,
+            full_spec(gain.shape),
+            full_spec(router.shape),
+            pl.BlockSpec((block, 1), lambda i: (i, 0)),
+            wide_spec,
+        ],
+        out_specs=[own_spec, pl.BlockSpec((block, half), lambda i: (jnp.minimum(i, 1), 0)), mixed, mixed],
+        out_shape=[
+            shape_of((seq // 2, width), WIDE),
+            shape_of((seq // 2, half), NARROW),
+            shape_of((seq, width), NARROW),
+            shape_of((seq, width), NARROW),
+        ],
+        scratch_shapes=[VMEM((2, block, half), NARROW)],
+        compiler_params=params(),
+        cost_estimate=cost(2 * seq * width * width, 5 * seq * width * 2),
+        name="hidden_rows",
+    )(place, *pieces, w_mine, w_other, tok_all, gain, router, route_all, grad_all)
+
+
+def expert_out_kernel(x, w_in, w_out, act, slope, out, total):
+    step = pl.program_id(0)
+    pre = dot_nn(x[...], w_in[...])
+    square = pre * pre
+    bent = jnp.tanh(0.7978845608028654 * pre * (1.0 + 0.044715 * square))
+    act_low = (0.5 * pre * (1.0 + bent)).astype(NARROW)
+    act[...] = act_low
+    inner = 0.7978845608028654 * (1.0 + 0.134145 * square)
+    slope[...] = (0.5 * (1.0 + bent) + 0.5 * pre * (1.0 - bent * bent) * inner).astype(NARROW)
+    piece = dot_nt(act_low, w_out[...])
+
+    @pl.when(step == 0)
+    def _():
+        total[...] = piece
+
+    @pl.when(step > 0)
+    def _():
+        total[...] += piece
+
+    @pl.when(step == pl.num_programs(0) - 1)
+    def _():
+        out[...] = total[...].astype(NARROW)
+
+
+def expert_back_kernel(g, slope, w_in, w_out, grad_pre, out, total):
+    step = pl.program_id(0)
+    low = (dot_nn(g[...], w_out[...]) * slope[...].astype(WIDE)).astype(NARROW)
+    grad_pre[...] = low
+    piece = dot_nt(low, w_in[...])
+
+    @pl.when(step == 0)
+    def _():
+        total[...] = piece
+
+    @pl.when(step > 0)
+    def _():
+        total[...] += piece
+
+    @pl.when(step == pl.num_programs(0) - 1)
+    def _():
+        out[...] = total[...].astype(NARROW)
+
+
+def expert_forward(x, w_in, w_out, block):
+    seq, width = x.shape
+    units = w_in.shape[1]
+    w_spec = pl.BlockSpec((width, block), lambda i: (0, i))
+    unit_spec = pl.BlockSpec((seq, block), lambda i: (0, i))
+    return pl.pallas_call(
+        expert_out_kernel,
+        grid=(units // block,),
+        in_specs=[full_spec(x.shape), w_spec, w_spec],
+        out_specs=[unit_spec, unit_spec, full_spec(x.shape)],
+        out_shape=[shape_of((seq, units), NARROW)] * 2 + [shape_of(x.shape, NARROW)],
+        scratch_shapes=[VMEM(x.shape, WIDE)],
+        compiler_params=params(),
+        cost_estimate=cost(4 * seq * width * units, 4 * seq * units),
+        name="expert_forward",
+    )(x, w_in, w_out)
+
+
+def expert_backward(g, slope, w_in, w_out, block):
+    seq, width = g.shape
+    units = w_in.shape[1]
+    w_spec = pl.BlockSpec((width, block), lambda i: (0, i))
+    unit_spec = pl.BlockSpec((seq, block), lambda i: (0, i))
+    return pl.pallas_call(
+        expert_back_kernel,
+        grid=(units // block,),
+        in_specs=[full_spec(g.shape), unit_spec, w_spec, w_spec],
+        out_specs=[unit_spec, full_spec(g.shape)],
+        out_shape=[shape_of((seq, units), NARROW), shape_of(g.shape, NARROW)],
+        scratch_shapes=[VMEM(g.shape, WIDE)],
+        compiler_params=params(),
+        cost_estimate=cost(4 * seq * width * units, 4 * seq * units),
+        name="expert_backward",
+    )(g, slope, w_in, w_out)
+
+
+def weight_grad_kernel(left, right, out):
+    out[...] = dot_tn(left[...], right[...]).astype(NARROW)
+
+
+def weight_grad(left, right, block):
+    seq, width = left.shape
+    units = right.shape[1]
+    return pl.pallas_call(
+        weight_grad_kernel,
+        grid=(units // block,),
+        in_specs=[full_spec(left.shape), pl.BlockSpec((seq, block), lambda i: (0, i))],
+        out_specs=pl.BlockSpec((width, block), lambda i: (0, i)),
+        out_shape=shape_of((width, units), NARROW),
+        compiler_params=params(),
+        cost_estimate=cost(2 * seq * width * units, 4 * seq * units),
+        name="weight_grad",
+    )(left, right)
+
+
+def combine_kernel(place, hidden, out_mine, out_got, rows_mine, rows_got, grad, route, gain, router, w_mine, att, output, grad_hidden, sums, back_own, back_send, w_grad, grad_y):
+    row, col = place[0], place[1]
+    block = out_mine.shape[0]
+    count = router.shape[0]
+    size = back_own.shape[1]
+    gain_wide = gain[...].astype(WIDE)
+    total = [jnp.zeros((1, gain_wide.shape[1]), WIDE) for _ in range(1 + count)]
+    for half in range(2):
+        part = pl.ds(half * block, block)
+        mine = col == half
+        expert_out = jnp.where(mine, out_mine[...].astype(WIDE), out_got[...].astype(WIDE))
+        grad_rows = jnp.where(mine, rows_mine[...].astype(WIDE), rows_got[...].astype(WIDE))
+        wide = hidden[part, :]
+        grad_wide = grad[part, :].astype(WIDE)
+        inverse = lax.rsqrt(jnp.mean(wide * wide, axis=-1, keepdims=True) + EPS)
+        scaled = wide * inverse
+        hn = scaled * gain_wide
+        probs, hots, gate = gate_values(hn, route[part, :], router)
+        output[part, :] = (wide + gate * expert_out).astype(NARROW)
+        grad_gate = jnp.sum(grad_wide * expert_out, axis=1, keepdims=True) * gate
+        grad_hn = grad_rows
+        for e in range(count):
+            grad_logit = grad_gate * (hots[e] - probs[e])
+            grad_hn = grad_hn + grad_logit * router[e : e + 1]
+            total[1 + e] += jnp.sum(hn * grad_logit, axis=0, keepdims=True)
+        total[0] += jnp.sum(grad_hn * scaled, axis=0, keepdims=True)
+        u = grad_hn * gain_wide
+        back = grad_wide + inverse * u - wide * (inverse * inverse * inverse) * jnp.mean(u * wide, axis=-1, keepdims=True)
+        grad_hidden[part, :] = back
+        low = back.astype(NARROW)
+        grad_y[part, :] = low
+        grad_att = dot_nn(low, w_mine[...]).astype(NARROW)
+
+        @pl.when(row == 0)
+        def _():
+            back_own[part, :] = grad_att[:, :size]
+            back_send[part, :] = grad_att[:, size:]
+
+        @pl.when(row == 1)
+        def _():
+            back_own[part, :] = grad_att[:, size:]
+            back_send[part, :] = grad_att[:, :size]
+
+    line = lax.broadcasted_iota(jnp.int32, sums.shape, 0)
+    packed = jnp.zeros(sums.shape, WIDE)
+    for e in range(1 + count):
+        packed = packed + jnp.where(line == e, total[e], 0.0)
+    sums[...] = packed
+    w_grad[...] = dot_tn(grad_y[...], att[...]).astype(NARROW)
+
+
+def combine(place, hidden, outs, backs, grad, route, gain, router, w_mine, att, size):
+    tokens, width = hidden.shape
+    half = w_mine.shape[1]
+    args = (place, hidden, *outs, *backs, grad, route, gain, router, w_mine, att)
+    shapes = [
+        shape_of((tokens, width), NARROW),
+        shape_of((tokens, width), WIDE),
+        shape_of((8, width), WIDE),
+        shape_of((tokens, size), NARROW),
+        shape_of((tokens, size), NARROW),
+        shape_of((width, half), NARROW),
+    ]
+    return pl.pallas_call(
+        combine_kernel,
+        in_specs=[smem_spec()] + [pl.BlockSpec(memory_space=VMEM)] * (len(args) - 1),
+        out_specs=[pl.BlockSpec(memory_space=VMEM)] * len(shapes),
+        out_shape=shapes,
+        scratch_shapes=[VMEM((tokens, width), NARROW)],
+        compiler_params=params(),
+        cost_estimate=cost(4 * tokens * width * half, 8 * tokens * width * 2),
+        name="combine",
+    )(*args)
+
+
+def project_back_kernel(g, normed, w_all, tok, sums, w_grad, grad_normed):
+    seq = g.shape[0]
+    cols = g.shape[1]
+    width = tok.shape[1]
+    total = jnp.zeros((1, width), WIDE)
+    block = seq // 4
+    for i in range(4):
+        part = pl.ds(i * block, block)
+        back = dot_nt(g[part, :], w_all[...])
+        rows = tok[part, :].astype(WIDE)
+        inverse = lax.rsqrt(jnp.mean(rows * rows, axis=-1, keepdims=True) + EPS)
+        total = total + jnp.sum(back * rows * inverse, axis=0, keepdims=True)
+        grad_normed[pl.ds((i % 2) * 2 * block + (i // 2) * block, block), :] = back.astype(NARROW)
+    w_grad[:, :cols] = dot_tn(normed[...], g[...]).astype(NARROW)
+    line = lax.broadcasted_iota(jnp.int32, (128, width), 0)
+    lines = jnp.where(line == 0, total, 0.0)
+    for e in range(3):
+        lines = lines + jnp.where(line == 1 + e, sums[e : e + 1], 0.0)
+    w_grad[:, cols:] = lines.T[:, : w_grad.shape[1] - cols].astype(NARROW)
+
+
+def project_back(g, normed, w_all, tok_all, sums):
+    seq, width = tok_all.shape
+    cols = g.shape[1]
+    args = (g, normed, w_all, tok_all, sums)
+    return pl.pallas_call(
+        project_back_kernel,
+        in_specs=[pl.BlockSpec(memory_space=VMEM)] * len(args),
+        out_specs=[pl.BlockSpec(memory_space=VMEM)] * 2,
+        out_shape=[shape_of((width, cols + 64), NARROW), shape_of((seq, width), NARROW)],
+        compiler_params=params(),
+        cost_estimate=cost(4 * seq * width * cols, 4 * seq * width * 2),
+        name="project_back",
+    )(*args)
+
+
+def finish_kernel(place, tok, gain, grad_hidden, mine, got, out):
+    col = place[1]
+    block = mine.shape[0]
+    gain_wide = gain[...].astype(WIDE)
+    for half in range(2):
+        part = pl.ds(half * block, block)
+        grad_normed = jnp.where(col == half, mine[...].astype(WIDE), got[...].astype(WIDE))
+        rows = tok[part, :].astype(WIDE)
+        inverse = lax.rsqrt(jnp.mean(rows * rows, axis=-1, keepdims=True) + EPS)
+        u = grad_normed * gain_wide
+        out[part, :] = grad_hidden[part, :] + inverse * u - rows * (inverse * inverse * inverse) * jnp.mean(u * rows, axis=-1, keepdims=True)
+
+
+def finish(place, tok, gain, grad_hidden, mine, got):
+    args = (place, tok, gain, grad_hidden, mine, got)
+    return pl.pallas_call(
+        finish_kernel,
+        in_specs=[smem_spec()] + [pl.BlockSpec(memory_space=VMEM)] * (len(args) - 1),
+        out_specs=pl.BlockSpec(memory_space=VMEM),
+        out_shape=shape_of(tok.shape, WIDE),
+        compiler_params=params(),
+        cost_estimate=cost(tok.size * 16, tok.size * 12),
+        name="finish",
+    )(*args)
+
+
+def swap(value, axis, flip=1):
+    size = lax.axis_size(axis)
+    return lax.ppermute(value, axis, [(i, i ^ flip) for i in range(size)])
+
+
+def pick(value, index, axis=0):
+    return lax.dynamic_index_in_dim(value, index, axis, keepdims=False)
+
+
+def in_order(first, mine, got, axis=0):
+    return jnp.where(first, jnp.concatenate([mine, got], axis), jnp.concatenate([got, mine], axis))
+
+
+def from_other_row(value, col):
+    half = value.shape[0] // 2
+    got = swap(lax.dynamic_slice_in_dim(value, col * half, half, 0), "row")
+    return in_order(col == 0, got, swap(got, "col"))
+
+
+def sum_to_rows(part, col):
+    rows = part.shape[0]
+    halves = part.reshape(2, rows // 2, -1)
+    got = swap(pick(halves, 1 - col), "col")
+    both = (pick(halves, col).astype(WIDE) + got.astype(WIDE)).astype(NARROW).reshape(2, rows // 4, -1)
+    mine = (both[0].astype(WIDE) + swap(both[1], "row").astype(WIDE)).astype(NARROW)
+    return mine, swap(mine, "col")
+
+
+def add_low(a, b):
+    return (a.astype(WIDE) + b.astype(WIDE)).astype(NARROW)
+
+
+def scatter_dp(value, order):
+    count = lax.axis_size("dp")
+    place = lax.axis_index("dp")
+    bits = count.bit_length() - 1
+    rows = value.shape[0] // count
+    value = value.reshape((2,) * bits + (rows, value.shape[1]))
+    left = list(range(bits - 1, -1, -1))
+    for bit in order:
+        axis = left.index(bit)
+        at = (place >> bit) & 1
+        got = swap(pick(value, 1 - at, axis), "dp", 1 << bit)
+        value = add_low(pick(value, at, axis), got)
+        left.remove(bit)
+    return value
+
+
+def sum_dp(value):
+    count = lax.axis_size("dp")
+    flip = 1
+    while flip < count:
+        value = value + swap(value, "dp", flip)
+        flip *= 2
+    return value
+
+
+def local_pair(tokens, grad_out, routes, norm1_gain, w_query, w_key, w_value, w_output, rel_table, rel_bucket, norm2_gain, router, w_in, w_out):
+    tok_rows, width = tokens.shape
+    seq = 2 * tok_rows
+    row, col = lax.axis_index("row"), lax.axis_index("col")
+    place = jnp.stack([row, col]).astype(jnp.int32)
+    col_heads = H // lax.axis_size("col")
+    heads = col_heads // 2
+    size = w_query.shape[1] // col_heads
+    wide = heads * size
+
+    stacked = jnp.stack([w_query, w_key, w_value], 1).reshape(w_query.shape[0], 3, 2, wide)
+    w_own = pick(stacked, row, 2).reshape(w_query.shape[0], 3 * wide)
+    w_oth = swap(pick(stacked, 1 - row, 2).reshape(w_query.shape[0], 3 * wide), "row")
+    tok_all = jnp.concatenate([tokens, from_other_row(tokens, col)], 0)
+    gain_one, gain_two = norm1_gain[None, :], norm2_gain[None, :]
+
+    table = lax.dynamic_slice_in_dim(rel_table.astype(WIDE), col * col_heads + row * heads, heads, 1)
+    bucket = jnp.pad(rel_bucket[None, :], ((0, 0), (1, 0)), constant_values=-1)
+    router_lines = router.astype(WIDE).T
+
+    normed, q, k, v, w_all = project(place, tok_all, gain_one, w_own, w_oth, heads, size, 256)
+
+    grad_all = jnp.concatenate([grad_out, from_other_row(grad_out, col)], 0)
+    kinds = routes.astype(WIDE).reshape(-1, 128)
+    kinds_all = jnp.concatenate([kinds, swap(kinds, "row")], 0).reshape(seq, 1).astype(jnp.int32)
+    w_mine = in_order(row == 0, w_output, swap(w_output, "row"))
+    w_other = swap(w_mine, "col")
+
+    att, shares = attend(place, bucket, table, q, k, v, 256, 0, seq)
+    att_row = swap(att, "row")
+    pieces = (att, att_row, swap(att, "col"), swap(att_row, "col"))
+    hidden, att_own, rows, grads = hidden_rows(place, pieces, w_mine, w_other, tok_all, gain_two, router_lines, kinds_all, grad_all)
+
+    weight_in, weight_out = w_in[0], w_out[0]
+    act, slope, out_part = expert_forward(rows, weight_in, weight_out, 512)
+    grad_pre, rows_part = expert_backward(grads, slope, weight_in, weight_out, 512)
+    outs = sum_to_rows(out_part, col)
+    backs = sum_to_rows(rows_part, col)
+    grad_in = weight_grad(rows, grad_pre, 512)
+    grad_out_w = weight_grad(grads, act, 512)
+    grad_in_shard = scatter_dp(grad_in, (0, 1, 2)).astype(WIDE)
+    grad_out_shard = scatter_dp(grad_out_w, (1, 0, 2)).astype(WIDE)
+
+    output, grad_hidden, sums, back_own, back_send, grad_wo = combine(
+        place, hidden, outs, backs, grad_out, routes, gain_two, router_lines, w_mine, att_own, wide
+    )
+    back_oth = swap(back_send, "row")
+    keep = attend_back(place, bucket, q, k, v, shares[:, :tok_rows], back_own, 256, 0, None)
+    g, table_part = attend_back(place, bucket, q, k, v, shares[:, tok_rows:], back_oth, 256, tok_rows, keep)
+
+    w_part, normed_part = project_back(g, normed, w_all, tok_all, sums)
+    normed_sums = sum_to_rows(normed_part, col)
+    grad_tokens = finish(place, tokens, gain_one, grad_hidden, *normed_sums)
+
+    part = scatter_dp(jnp.concatenate([w_part, grad_wo], 1), (0, 1, 2))
+    per_row = part.shape[0] // 2
+    halves = part.reshape(2, per_row, -1)
+    mine, got = pick(halves, row).astype(WIDE), swap(pick(halves, 1 - row), "row").astype(WIDE)
+    wqkv = 3 * wide
+
+    def columns(i):
+        return in_order(row == 0, mine[:, i * wide : (i + 1) * wide], got[:, i * wide : (i + 1) * wide], 1)
+
+    small = mine[:, wqkv : wqkv + 4] + got[:, wqkv : wqkv + 4]
+    grads_gain_one = small[:, 0] + swap(small[:, 0], "col")
+    grads_output = mine[:, wqkv + 64 :] + got[:, wqkv + 64 :]
+
+    table_sum = sum_dp(table_part[:, :8])
+    grad_table = in_order(row == 0, table_sum[:, :heads], swap(table_sum, "row")[:, :heads], 1)
+    return (
+        output,
+        grad_tokens,
+        grads_gain_one,
+        columns(0),
+        columns(1),
+        columns(2),
+        grads_output,
+        grad_table,
+        small[:, 1],
+        small[:, 2:4],
+        grad_in_shard[None],
+        grad_out_shard[None],
+    )
+
+
 def solution(mesh):
     in_specs = (
         P(("dp", "row"), None),
@@ -325,4 +1075,5 @@
         P("row", "dp", "col"),
         P("row", "dp", "col"),
     )
-    return jax.shard_map(local, mesh=mesh, in_specs=in_specs, out_specs=out_specs, check_vma=False)
+    paired = mesh.shape["row"] == 2 and mesh.shape["col"] == 2
+    return jax.shard_map(local_pair if paired else local, mesh=mesh, in_specs=in_specs, out_specs=out_specs, check_vma=False)

time: 1610 us -> 242 us (0.15); the launches traced: 1590 us -> 241 us
  local copies, waits for them, and re-layouts: 872 us -> 25.2 us
  waiting for transfers between devices: 353 us -> 71.1 us
  blocking collectives: 175 us -> 0 us
  matrix products: 99.8 us -> 0 us
  Pallas kernels: 0 us -> 85 us
  other arithmetic: 56.6 us -> 23.4 us
  starting transfers between devices: 14.8 us -> 35.2 us
    unnamed x151 -> x56, local copies, waits for them, and re-layouts: 802 us -> 5.13 us
    reduce_scatter x8 -> x0, waiting for transfers between devices: 297 us -> none  [the longest x1 129 us: local(): lax.psum_scatter(grad_w_key, ('dp', 'row'), scatter_dimension=0, tiled=True)]
    dot_general x28 -> x0, matrix products: 95.6 us -> none  [the longest x6 21.1 us: contract_rows(): lax.dot_general(left, right, (((0,), (0,)), ((), ())), preferred_element_...]
    pallas_call x0 -> x12, Pallas kernels: none -> 85 us  [the longest x2 18.8 us: attend_back(): pl.pallas_call(kernel, grid=(rows // block,), in_specs=in_specs, out_spec...]
    unnamed x1 -> x0, blocking collectives: 76.1 us -> none
    ppermute x0 -> x36, waiting for transfers between devices: none -> 71.1 us  [swap(): return lax.ppermute(value, axis, [(i, i ^ flip) for i in range(size)])]
    all_gather x6 -> x0, blocking collectives: 54.8 us -> none  [the longest x1 10.9 us: local(): lax.all_gather(w_query, 'row', axis=0, tiled=True)]
    all_to_all x3 -> x0, waiting for transfers between devices: 36.5 us -> none  [the longest x1 16.2 us: local(): lax.all_to_all(out_sum.astype(NARROW).reshape(n_exp, capacity, width), 'r...]
  transfers between devices with their start and end apart: 14 -> 36, of which waited for: 9 -> 13; matrix products, arithmetic and copies ran while one was open for 31% -> 18% of each run, Pallas kernels for 0% -> 21%
where the time goes in v1:
time: 242 us; the launch traced here: 241 us
  Pallas kernels  85 us (35%)
  waiting for transfers between devices  71.1 us (29%)
  starting transfers between devices  35.2 us (15%)
  local copies, waits for them, and re-layouts  25.2 us (10%)
  other arithmetic  23.4 us (10%)
    ppermute x36, waiting for transfers between devices, swap(): return lax.ppermute(value, axis, [(i, i ^ flip) for i in range(size)])  71.1 us
    ppermute x36, starting transfers between devices, swap(): return lax.ppermute(value, axis, [(i, i ^ flip) for i in range(size)])  35.2 us
    pallas_call x2, Pallas kernels, attend_back(): pl.pallas_call(kernel, grid=(rows // block,), in_specs=in_specs, out_spec...  18.8 us
    pallas_call x1, Pallas kernels, expert_forward(): pl.pallas_call(expert_out_kernel, grid=(units // block,), in_specs=[full_...  11.5 us
    pallas_call x1, Pallas kernels, attend(): pl.pallas_call(functools.partial(attend_kernel, begin // TILE), grid=(row...  11.2 us
    pallas_call x1, Pallas kernels, expert_backward(): pl.pallas_call(expert_back_kernel, grid=(units // block,), in_specs=[full...  9.53 us
    pallas_call x2, Pallas kernels, weight_grad(): pl.pallas_call(weight_grad_kernel, grid=(units // block,), in_specs=[full...  9.29 us
    pallas_call x1, Pallas kernels, hidden_rows(): pl.pallas_call(hidden_kernel, grid=(4,), in_specs=[smem_spec(), plain, tu...  7.33 us
  transfers between devices with their start and end apart: 36, of which 13 were waited for; matrix products, arithmetic and copies ran while one was open for 18% of the time, Pallas kernels for 21%

profile of v1, /device:TPU:0, one launch (start us, length us, event | category | flops | bytes accessed | tf_op | source)
XLA Modules:
  0.0 241.1 jit_solution(13953744848351476653)
XLA Ops:
  1.8 3.0 %collective-permute-start = (bf16[256,768]{1,0:T(8,128)(2,1)S(1)}, bf16[256,768]{1,0:T(8,128)(2,1)S(1)}, u32[]{:S(2)}, u32[]{:S(2)}) collective-permute-start(bf16[256,768]{1,0:T(8,128)(2,1)S(1)} %constant_dynamic-slice_fusion.9), channel_id=1, source_target_pairs={{0,2},{2,0},{1,3},{3,1},{4,6},{6,4},{5,7},{7,5},{8,10},{10,8},{9,1... | collective-permute-start | bytes 1179656 | tf_op jit(solution)/shard_map/ppermute | solution.py:907
  8.5 2.0 collective-permute-start.9
  10.6 2.0 collective-permute-start.8
  12.6 2.2 collective-permute-done
  16.2 23.1 %collective-permute-done.8 = f32[4,128]{1,0:T(4,128)S(1)} collective-permute-done((f32[4,128]{1,0:T(4,128)S(1)}, f32[4,128]{1,0:T(4,128)S(1)}, u32[]{:S(2)}, u32[]{:S(2)}) %collective-permute-start.8) | collective-permute-done | bytes 2080 | tf_op jit(solution)/shard_map/ppermute | solution.py:907
  39.7 1.3 maximum_select_fusion
  42.2 4.2 %project.1 = (bf16[1024,768]{1,0:T(8,128)(2,1)S(1)}, bf16[3,1024,64]{2,1,0:T(8,128)(2,1)S(1)}, bf16[3,1024,64]{2,1,0:T(8,128)(2,1)S(1)}, bf16[3,1024,64]{2,1,0:T(8,128)(2,1)S(1)}, bf16[768,576]{1,0:T(8,128)(2,1)S(1)}) custom-call(s32[2]{0:T(128)S(1)} %pad_add_fusion.place.refs_0_, bf16[1024,768]{1,0:T(8,128)(2,1)} %pad_maximum_fusion.tok, ...), custom_call_target="tpu_custom_call" | custom-call | flops 905969664 | bytes 6291456 | tf_op jit(solution)/shard_map/project/pallas_call | solution.py:370
  46.5 11.2 %attend.1 = (bf16[1024,192]{1,0:T(8,128)(2,1)S(1)}, bf16[3,1024,1024]{2,1,0:T(8,128)(2,1)}) custom-call(s32[2]{0:T(128)S(1)} %pad_add_fusion.place.refs_0_, s32[1,2048]{1,0:T(1,128)S(1)} %pad.4.bucket.refs_1_, f32[32,3]{1,0:T(8,128)S(1)} %copy.110.table, bf16[3,1024,64]{2,1,0:T(8,128)(2,1)S(1)} %get-tuple-element.42.q.refs_2_, ...), custom_call_target="tpu_custom_call" | custom-call | flops 3221225472 | bytes 12582912 | tf_op jit(solution)/shard_map/attend/pallas_call | solution.py:426
  57.7 1.7 collective-permute-start.3
  59.4 1.5 maximum_select_fusion.2.w_mine
  64.1 7.9 %collective-permute-done.3.a_row = bf16[1024,192]{1,0:T(8,128)(2,1)S(1)} collective-permute-done((bf16[1024,192]{1,0:T(8,128)(2,1)S(1)}, bf16[1024,192]{1,0:T(8,128)(2,1)S(1)}, u32[]{:S(2)}, u32[]{:S(2)}) %collective-permute-start.3) | collective-permute-done | bytes 393248 | tf_op jit(solution)/shard_map/ppermute | solution.py:907
  72.0 6.9 %fusion.17 = (bf16[3,512,1024]{2,1,0:T(8,128)(2,1)}, bf16[3,512,1024]{2,1,0:T(8,128)(2,1)}) fusion(bf16[3,1024,1024]{2,1,0:T(8,128)(2,1)} %get-tuple-element.55), kind=kLoop, calls=%fused_computation.79 | loop fusion | bytes 12582912 | tf_op jit(solution)/shard_map/slice | solution.py:1009
  78.9 7.3 %hidden_rows.1 = (f32[512,768]{1,0:T(8,128)S(1)}, bf16[512,384]{1,0:T(8,128)(2,1)S(1)}, bf16[1024,768]{1,0:T(8,128)(2,1)}, bf16[1024,768]{1,0:T(8,128)(2,1)}) custom-call(s32[2]{0:T(128)S(1)} %pad_add_fusion.place.refs_0_, bf16[1024,192]{1,0:T(8,128)(2,1)S(1)} %get-tuple-element.45.a_mine, bf16[1024,192]{1,0:T(8,128)(2,1)S(1)} %collective-permute-done.3.a_row, ...), custom_call_target="tpu_custom_call" | custom-call | flops 1207959552 | bytes 7864320 | tf_op jit(solution)/shard_map/hidden_rows/pallas_call | solution.py:639
  87.4 1.4 copy-done.6
  88.8 11.5 %expert_forward.1 = (bf16[1024,1536]{1,0:T(8,128)(2,1)}, bf16[1024,1536]{1,0:T(8,128)(2,1)}, bf16[1024,768]{1,0:T(8,128)(2,1)S(1)}) custom-call(bf16[1024,768]{1,0:T(8,128)(2,1)S(1)} %copy-done.6, bf16[768,1536]{1,0:T(8,128)(2,1)S(1)} %bitcast.117, bf16[768,1536]{1,0:T(8,128)(2,1)} %bitcast.133), custom_call_target="tpu_custom_call" | custom-call | flops 4831838208 | bytes 6291456 | tf_op jit(solution)/shard_map/expert_forward/pallas_call | solution.py:718
  100.3 4.7 %weight_grad.3 = bf16[768,1536]{1,0:T(8,128)(2,1)S(1)} custom-call(bf16[1024,768]{1,0:T(8,128)(2,1)S(1)} %copy-done.8, bf16[1024,1536]{1,0:T(8,128)(2,1)} %get-tuple-element.71.right), custom_call_target="tpu_custom_call" | custom-call | flops 2415919104 | bytes 6291456 | tf_op jit(solution)/shard_map/weight_grad/pallas_call | solution.py:756
  105.0 9.5 %expert_backward.1 = (bf16[1024,1536]{1,0:T(8,128)(2,1)}, bf16[1024,768]{1,0:T(8,128)(2,1)S(1)}) custom-call(bf16[1024,768]{1,0:T(8,128)(2,1)S(1)} %copy-done.9, bf16[1024,1536]{1,0:T(8,128)(2,1)} %get-tuple-element.50.slope, bf16[768,1536]{1,0:T(8,128)(2,1)S(1)} %bitcast.118, bf16[768,1536]{1,0:T(8,128)(2,1)} %bitcast.134), custom_call_target="tpu_custom_call" | custom-call | flops 4831838208 | bytes 6291456 | tf_op jit(solution)/shard_map/expert_backward/pallas_call | solution.py:736
  118.4 1.8 collective-permute-start.33
  121.1 4.6 %weight_grad.2 = bf16[768,1536]{1,0:T(8,128)(2,1)S(1)} custom-call(bf16[1024,768]{1,0:T(8,128)(2,1)S(1)} %copy-done.7, bf16[1024,1536]{1,0:T(8,128)(2,1)} %get-tuple-element.70.right), custom_call_target="tpu_custom_call" | custom-call | flops 2415919104 | bytes 6291456 | tf_op jit(solution)/shard_map/weight_grad/pallas_call | solution.py:756
  126.0 1.6 collective-permute-start.30
  127.6 1.3 fusion.4
  129.0 1.6 collective-permute-start.15
  130.6 1.3 fusion.5
  132.5 14.1 %collective-permute-done.33 = bf16[2,2,96,1536]{3,2,0,1:T(8,128)(2,1)} collective-permute-done((bf16[2,2,96,1536]{3,2,0,1:T(8,128)(2,1)}, bf16[2,2,96,1536]{3,2,0,1:T(8,128)(2,1)}, u32[]{:S(2)}, u32[]{:S(2)}) %collective-permute-start.33) | collective-permute-done | bytes 1179680 | tf_op jit(solution)/shard_map/ppermute | solution.py:907
  146.6 1.5 fusion
  148.2 1.7 collective-permute-start.34
  150.8 4.0 %collective-permute-done.30 = bf16[2,2,96,1536]{3,2,0,1:T(8,128)(2,1)S(1)} collective-permute-done((bf16[2,2,96,1536]{3,2,0,1:T(8,128)(2,1)S(1)}, bf16[2,2,96,1536]{3,2,0,1:T(8,128)(2,1)S(1)}, u32[]{:S(2)}, u32[]{:S(2)}) %collective-permute-start.30) | collective-permute-done | bytes 1179680 | tf_op jit(solution)/shard_map/ppermute | solution.py:907
  155.5 6.0 %combine.1 = (bf16[512,768]{1,0:T(8,128)(2,1)}, f32[512,768]{1,0:T(8,128)}, f32[8,768]{1,0:T(8,128)S(1)}, bf16[512,192]{1,0:T(8,128)(2,1)S(1)}, bf16[512,192]{1,...) custom-call(s32[2]{0:T(128)S(1)} %pad_add_fusion.place.refs_0_, f32[512,768]{1,0:T(8,128)} %copy-done.3, ...), custom_call_target="tpu_custom_call" | custom-call | flops 603979776 | bytes 6291456 | tf_op jit(solution)/shard_map/combine/pallas_call | solution.py:831
  161.5 1.8 collective-permute-start.17
  163.2 8.1 %attend_back.2 = (bf16[512,192]{1,0:T(8,128)(2,1)S(1)}, f32[3,64,1024]{2,1,0:T(8,128)S(1)}, f32[3,64,1024]{2,1,0:T(8,128)S(1)}, f32[3,128,2048]{2,1,0:T(8,128)}) custom-call(s32[2]{0:T(128)S(1)} %pad_add_fusion.place.refs_0_, s32[1,2048]{1,0:T(1,128)S(1)} %pad.4.bucket.refs_1_, bf16[3,1024,64]{2,1,0:T(8,128)(2,1)S(1)} %get-tuple-element.42.q.refs_2_, ...), custom_call_target="tpu_custom_call" | custom-call | flops 2818572288 | bytes 6291456 | tf_op jit(solution)/shard_map/attend_back/pallas_call | solution.py:568
  171.6 2.7 %collective-permute-start.35 = (bf16[96,1536]{1,0:T(8,128)(2,1)S(1)}, bf16[96,1536]{1,0:T(8,128)(2,1)}, u32[]{:S(2)}, u32[]{:S(2)}) collective-permute-start(bf16[96,1536]{1,0:T(8,128)(2,1)S(1)} %dynamic-slice_bitcast_fusion.6), channel_id=1, source_target_pairs={{0,16},{4,20},{8,24},{12,28},{16,0},{20,4},{24,8},{28,12},{1,17},{... | collective-permute-start | bytes 884744 | tf_op jit(solution)/shard_map/ppermute | solution.py:907
  174.2 10.6 %attend_back.3 = (bf16[1024,576]{1,0:T(8,128)(2,1)S(1)}, f32[32,128]{1,0:T(8,128)S(1)}) custom-call(s32[2]{0:T(128)S(1)} %pad_add_fusion.place.refs_0_, s32[1,2048]{1,0:T(1,128)S(1)} %pad.4.bucket.refs_1_, bf16[3,1024,64]{2,1,0:T(8,128)(2,1)S(1)} %get-tuple-element.42.q.refs_2_, bf16[3,1024,64]{2,1,0:T(8,128)(2,1)S(1)} %get-tuple-element.43.k.refs_3_, ...), custom_call_target="tpu_custom_call" | custom-call | flops 2818572288 | bytes 6291456 | tf_op jit(solution)/shard_map/attend_back/pallas_call | solution.py:568
  184.9 1.6 collective-permute-start.26
  186.4 4.8 %project_back.1 = (bf16[768,640]{1,0:T(8,128)(2,1)S(1)}, bf16[1024,768]{1,0:T(8,128)(2,1)S(1)}) custom-call(bf16[1024,576]{1,0:T(8,128)(2,1)S(1)} %get-tuple-element.62.g, bf16[1024,768]{1,0:T(8,128)(2,1)} %copy-done.10, bf16[768,576]{1,0:T(8,128)(2,1)S(1)} %copy-done.12, bf16[1024,768]{1,0:T(8,128)(2,1)} %pad_maximum_fusion.tok, ...), custom_call_target="tpu_custom_call" | custom-call | flops 1811939328 | bytes 6291456 | tf_op jit(solution)/shard_map/project_back/pallas_call | solution.py:868
  194.0 1.6 collective-permute-start.27
  198.9 2.6 %collective-permute-start.32 = (bf16[96,1536]{1,0:T(8,128)(2,1)}, bf16[96,1536]{1,0:T(8,128)(2,1)}, u32[]{:S(2)}, u32[]{:S(2)}) collective-permute-start(bf16[96,1536]{1,0:T(8,128)(2,1)} %dynamic-slice_bitcast_fusion.7), channel_id=1, source_target_pairs={{0,16},{4,20},{8,24},{12,28},{16,0},{20,4},{24,8},{28,12},{1,17},{... | collective-permute-start | bytes 884744 | tf_op jit(solution)/shard_map/ppermute | solution.py:907
  201.5 2.5 %collective-permute-done.28 = f32[32,8]{1,0:T(8,128)S(1)} collective-permute-done((f32[32,8]{1,0:T(8,128)S(1)}, f32[32,8]{1,0:T(8,128)S(1)}, u32[]{:S(2)}, u32[]{:S(2)}) %collective-permute-start.28) | collective-permute-done | bytes 1056 | tf_op jit(solution)/shard_map/ppermute | solution.py:907
  205.5 2.2 collective-permute-done.29
  208.4 1.9 fusion.15
  211.4 1.4 fusion.2
  212.9 1.6 collective-permute-start.22
  216.5 1.9 fusion.13
  218.3 3.0 %collective-permute-done.22 = bf16[2,96,1024]{2,1,0:T(8,128)(2,1)S(1)} collective-permute-done((bf16[2,96,1024]{2,1,0:T(8,128)(2,1)S(1)}, bf16[2,96,1024]{2,1,0:T(8,128)(2,1)S(1)}, u32[]{:S(2)}, u32[]{:S(2)}) %collective-permute-start.22) | collective-permute-done | bytes 393248 | tf_op jit(solution)/shard_map/ppermute | solution.py:907
  222.7 1.3 collective-permute-done.19
  224.2 6.0 %collective-permute-done.23 = bf16[96,1024]{1,0:T(8,128)(2,1)S(1)} collective-permute-done((bf16[96,1024]{1,0:T(8,128)(2,1)S(1)}, bf16[96,1024]{1,0:T(8,128)(2,1)S(1)}, u32[]{:S(2)}, u32[]{:S(2)}) %collective-permute-start.23) | collective-permute-done | bytes 196640 | tf_op jit(solution)/shard_map/ppermute | solution.py:907
  230.3 2.0 collective-permute-start.24
  232.4 2.6 %collective-permute-done.24 = bf16[48,1024]{1,0:T(8,128)(2,1)S(1)} collective-permute-done((bf16[48,1024]{1,0:T(8,128)(2,1)S(1)}, bf16[48,1024]{1,0:T(8,128)(2,1)S(1)}, u32[]{:S(2)}, u32[]{:S(2)}) %collective-permute-start.24) | collective-permute-done | bytes 98336 | tf_op jit(solution)/shard_map/ppermute | solution.py:907
  238.6 2.4 %finish.1 = f32[512,768]{1,0:T(8,128)} custom-call(s32[2]{0:T(128)S(1)} %pad_add_fusion.place.refs_0_, bf16[512,768]{1,0:T(8,128)(2,1)S(1)} %copy-done, bf16[1,768]{1,0:T(2,128)(2,1)S(1)} %broadcast_in_dim.22.gain, f32[512,768]{1,0:T(8,128)S(1)} %copy-done.2, bf16[256,768]{1,0:T(8,128)(2,1)S(1)} %add_convert_fusion.mine, ...), custom_call_target="tpu_custom_call" | custom-call | flops 6291456 | bytes 4718592 | tf_op jit(solution)/shard_map/finish/pallas_call | solution.py:894
  (163 shorter events, 36.0 us)
Async XLA Ops:
  1.8 13.0 %collective-permute-start = (bf16[256,768]{1,0:T(8,128)(2,1)S(1)}, bf16[256,768]{1,0:T(8,128)(2,1)S(1)}, u32[]{:S(2)}, u32[]{:S(2)}) collective-permute-start(bf16[256,768]{1,0:T(8,128)(2,1)S(1)} %constant_dynamic-slice_fusion.9), channel_id=1, source_target_pairs={{0,2},{2,0},{1,3},{3,1},{4,6},{6,4},{5,7},{7,5},{8,10},{10,8},{9,1... | collective-permute-start | bytes 1179656 | tf_op jit(solution)/shard_map/ppermute | solution.py:907
  6.7 9.3 %copy-start.23 = (bf16[768]{0:T(1024)(128)(2,1)S(1)}, bf16[768]{0:T(1024)(128)(2,1)}, u32[]{:S(2)}) copy-start(bf16[768]{0:T(1024)(128)(2,1)} %param.17) | copy-start | bytes 4612
  6.7 9.4 %copy-start.24 = (bf16[768]{0:T(1024)(128)(2,1)S(1)}, bf16[768]{0:T(1024)(128)(2,1)}, u32[]{:S(2)}) copy-start(bf16[768]{0:T(1024)(128)(2,1)} %param.24) | copy-start | bytes 4612
  6.7 9.4 %copy-start.21 = (s32[2047]{0:T(1024)S(1)}, s32[2047]{0:T(1024)}, u32[]{:S(2)}) copy-start(s32[2047]{0:T(1024)} %param.23) | copy-start | bytes 24568
  7.7 34.5 %collective-permute-start.2 = (bf16[384,576]{1,0:T(8,128)(2,1)}, bf16[384,576]{1,0:T(8,128)(2,1)}, u32[]{:S(2)}, u32[]{:S(2)}) collective-permute-start(bf16[384,576]{1,0:T(8,128)(2,1)} %copy.95), channel_id=1, source_target_pairs={{0,2},{2,0},{1,3},{3,1},{4,6},{6,4},{5,7},{7,5},{8,10},{10,8},{9,1... | collective-permute-start | bytes 1327112 | tf_op jit(solution)/shard_map/ppermute | solution.py:907
  8.5 31.0 %collective-permute-start.9 = (bf16[256,768]{1,0:T(8,128)(2,1)}, bf16[256,768]{1,0:T(8,128)(2,1)}, u32[]{:S(2)}, u32[]{:S(2)}) collective-permute-start(bf16[256,768]{1,0:T(8,128)(2,1)} %constant_dynamic-slice_fusion.6), channel_id=1, source_target_pairs={{0,2},{2,0},{1,3},{3,1},{4,6},{6,4},{5,7},{7,5},{8,10},{10,8},{9,1... | collective-permute-start | bytes 1179656 | tf_op jit(solution)/shard_map/ppermute | solution.py:907
  10.5 48.9 %collective-permute-start.6 = (bf16[384,384]{1,0:T(8,128)(2,1)}, bf16[384,384]{1,0:T(8,128)(2,1)}, u32[]{:S(2)}, u32[]{:S(2)}) collective-permute-start(bf16[384,384]{1,0:T(8,128)(2,1)} %param.21), channel_id=1, source_target_pairs={{0,2},{2,0},{1,3},{3,1},{4,6},{6,4},{5,7},{7,5},{8,10},{10,8},{9,1... | collective-permute-start | bytes 884744 | tf_op jit(solution)/shard_map/ppermute | solution.py:907
  10.6 28.7 %collective-permute-start.8 = (f32[4,128]{1,0:T(4,128)S(1)}, f32[4,128]{1,0:T(4,128)S(1)}, u32[]{:S(2)}, u32[]{:S(2)}) collective-permute-start(f32[4,128]{1,0:T(4,128)S(1)} %bitcast.131), channel_id=1, source_target_pairs={{0,2},{2,0},{1,3},{3,1},{4,6},{6,4},{5,7},{7,5},{8,10},{10,8},{9,1... | collective-permute-start | bytes 6152 | tf_op jit(solution)/shard_map/ppermute | solution.py:907
  14.7 24.9 %collective-permute-start.1 = (bf16[256,768]{1,0:T(8,128)(2,1)S(1)}, bf16[256,768]{1,0:T(8,128)(2,1)}, u32[]{:S(2)}, u32[]{:S(2)}) collective-permute-start(bf16[256,768]{1,0:T(8,128)(2,1)S(1)} %collective-permute-done), channel_id=1, source_target_pairs={{0,1},{1,0},{2,3},{3,2},{4,5},{5,4},{6,7},{7,6},{8,9},{9,8},{10,11... | collective-permute-start | bytes 1179656 | tf_op jit(solution)/shard_map/ppermute | solution.py:907
  15.7 25.3 %copy-start = (bf16[512,768]{1,0:T(8,128)(2,1)S(1)}, bf16[512,768]{1,0:T(8,128)(2,1)}, u32[]{:S(2)}) copy-start(bf16[512,768]{1,0:T(8,128)(2,1)} %tok.1) | copy-start | bytes 2359300
  39.6 22.0 %collective-permute-start.10 = (bf16[256,768]{1,0:T(8,128)(2,1)}, bf16[256,768]{1,0:T(8,128)(2,1)S(1)}, u32[]{:S(2)}, u32[]{:S(2)}) collective-permute-start(bf16[256,768]{1,0:T(8,128)(2,1)} %collective-permute-done.9), channel_id=1, source_target_pairs={{0,1},{1,0},{2,3},{3,2},{4,5},{5,4},{6,7},{7,6},{8,9},{9,8},{10,11... | collective-permute-start | bytes 1179656 | tf_op jit(solution)/shard_map/ppermute | solution.py:907
  46.5 11.2 %copy-start.10 = (bf16[1024,768]{1,0:T(8,128)(2,1)}, bf16[1024,768]{1,0:T(8,128)(2,1)S(1)}, u32[]{:S(2)}) copy-start(bf16[1024,768]{1,0:T(8,128)(2,1)S(1)} %get-tuple-element.63.normed) | copy-start | bytes 4718596
  46.5 11.2 %copy-start.11 = (bf16[768,576]{1,0:T(8,128)(2,1)}, bf16[768,576]{1,0:T(8,128)(2,1)S(1)}, u32[]{:S(2)}) copy-start(bf16[768,576]{1,0:T(8,128)(2,1)S(1)} %get-tuple-element.64.w_all) | copy-start | bytes 2654212
  57.7 14.3 %collective-permute-start.3 = (bf16[1024,192]{1,0:T(8,128)(2,1)S(1)}, bf16[1024,192]{1,0:T(8,128)(2,1)S(1)}, u32[]{:S(2)}, u32[]{:S(2)}) collective-permute-start(bf16[1024,192]{1,0:T(8,128)(2,1)S(1)} %get-tuple-element.45.a_mine), channel_id=1, source_target_pairs={{0,2},{2,0},{1,3},{3,1},{4,6},{6,4},{5,7},{7,5},{8,10},{10,8},{9,1... | collective-permute-start | bytes 1179656 | tf_op jit(solution)/shard_map/ppermute | solution.py:907
  61.0 17.9 %collective-permute-start.7 = (bf16[768,384]{1,0:T(8,128)(2,1)S(1)}, bf16[768,384]{1,0:T(8,128)(2,1)S(1)}, u32[]{:S(2)}, u32[]{:S(2)}) collective-permute-start(bf16[768,384]{1,0:T(8,128)(2,1)S(1)} %maximum_select_fusion.2.w_mine), channel_id=1, source_target_pairs={{0,1},{1,0},{2,3},{3,2},{4,5},{5,4},{6,7},{7,6},{8,9},{9,8},{10,11... | collective-permute-start | bytes 1769480 | tf_op jit(solution)/shard_map/ppermute | solution.py:907
  61.2 17.7 %collective-permute-start.4 = (bf16[1024,192]{1,0:T(8,128)(2,1)S(1)}, bf16[1024,192]{1,0:T(8,128)(2,1)S(1)}, u32[]{:S(2)}, u32[]{:S(2)}) collective-permute-start(bf16[1024,192]{1,0:T(8,128)(2,1)S(1)} %get-tuple-element.45.a_mine), channel_id=1, source_target_pairs={{0,1},{1,0},{2,3},{3,2},{4,5},{5,4},{6,7},{7,6},{8,9},{9,8},{10,11... | collective-permute-start | bytes 1179656 | tf_op jit(solution)/shard_map/ppermute | solution.py:907
  72.0 6.9 %collective-permute-start.5 = (bf16[1024,192]{1,0:T(8,128)(2,1)S(1)}, bf16[1024,192]{1,0:T(8,128)(2,1)S(1)}, u32[]{:S(2)}, u32[]{:S(2)}) collective-permute-start(bf16[1024,192]{1,0:T(8,128)(2,1)S(1)} %collective-permute-done.3.a_row), channel_id=1, source_target_pairs={{0,1},{1,0},{2,3},{3,2},{4,5},{5,4},{6,7},{7,6},{8,9},{9,8},{10,11... | collective-permute-start | bytes 1179656 | tf_op jit(solution)/shard_map/ppermute | solution.py:907
  88.8 11.5 %copy-start.8 = (bf16[1024,768]{1,0:T(8,128)(2,1)S(1)}, bf16[1024,768]{1,0:T(8,128)(2,1)}, u32[]{:S(2)}) copy-start(bf16[1024,768]{1,0:T(8,128)(2,1)} %get-tuple-element.49.g.left) | copy-start | bytes 4718596
  115.5 12.1 %collective-permute-start.14 = (bf16[512,768]{1,0:T(8,128)(2,1)}, bf16[512,768]{1,0:T(8,128)(2,1)}, u32[]{:S(2)}, u32[]{:S(2)}) collective-permute-start(bf16[512,768]{1,0:T(8,128)(2,1)} %dynamic-slice_bitcast_fusion.1), channel_id=1, source_target_pairs={{0,1},{1,0},{2,3},{3,2},{4,5},{5,4},{6,7},{7,6},{8,9},{9,8},{10,11... | collective-permute-start | bytes 2359304 | tf_op jit(solution)/shard_map/ppermute | solution.py:907
  118.4 28.2 %collective-permute-start.33 = (bf16[2,2,96,1536]{3,2,0,1:T(8,128)(2,1)}, bf16[2,2,96,1536]{3,2,0,1:T(8,128)(2,1)}, u32[]{:S(2)}, u32[]{:S(2)}) collective-permute-start(bf16[2,2,96,1536]{3,2,0,1:T(8,128)(2,1)} %bitcast.102), channel_id=1, source_target_pairs={{0,8},{4,12},{8,0},{12,4},{16,24},{20,28},{24,16},{28,20},{1,9},{5... | collective-permute-start | bytes 3538952 | tf_op jit(solution)/shard_map/ppermute | solution.py:907
  121.1 9.5 %collective-permute-start.11 = (bf16[512,768]{1,0:T(8,128)(2,1)}, bf16[512,768]{1,0:T(8,128)(2,1)}, u32[]{:S(2)}, u32[]{:S(2)}) collective-permute-start(bf16[512,768]{1,0:T(8,128)(2,1)} %dynamic-slice_bitcast_fusion.2), channel_id=1, source_target_pairs={{0,1},{1,0},{2,3},{3,2},{4,5},{5,4},{6,7},{7,6},{8,9},{9,8},{10,11... | collective-permute-start | bytes 2359304 | tf_op jit(solution)/shard_map/ppermute | solution.py:907
  126.0 28.8 %collective-permute-start.30 = (bf16[2,2,96,1536]{3,2,0,1:T(8,128)(2,1)S(1)}, bf16[2,2,96,1536]{3,2,0,1:T(8,128)(2,1)S(1)}, u32[]{:S(2)}, u32[]{:S(2)}) collective-permute-start(bf16[2,2,96,1536]{3,2,0,1:T(8,128)(2,1)S(1)} %bitcast.125), channel_id=1, source_target_pairs={{0,4},{4,0},{8,12},{12,8},{16,20},{20,16},{24,28},{28,24},{1,5},{5... | collective-permute-start | bytes 3538952 | tf_op jit(solution)/shard_map/ppermute | solution.py:907
  128.9 17.7 %copy-start.13 = (bf16[2,1,2,96,1536]{4,3,2,1,0:T(8,128)(2,1)S(1)}, bf16[2,1,2,96,1536]{4,3,2,1,0:T(8,128)(2,1)}, u32[]{:S(2)}) copy-start(bf16[2,1,2,96,1536]{4,3,2,1,0:T(8,128)(2,1)} %get-tuple-element.136) | copy-start | bytes 3538948
  129.0 21.0 %collective-permute-start.15 = (bf16[256,768]{1,0:T(8,128)(2,1)S(1)}, bf16[256,768]{1,0:T(8,128)(2,1)S(1)}, u32[]{:S(2)}, u32[]{:S(2)}) collective-permute-start(bf16[256,768]{1,0:T(8,128)(2,1)S(1)} %slice.106), channel_id=1, source_target_pairs={{0,2},{2,0},{1,3},{3,1},{4,6},{6,4},{5,7},{7,5},{8,10},{10,8},{9,1... | collective-permute-start | bytes 1179656 | tf_op jit(solution)/shard_map/ppermute | solution.py:907
  131.9 18.2 %collective-permute-start.12 = (bf16[256,768]{1,0:T(8,128)(2,1)S(1)}, bf16[256,768]{1,0:T(8,128)(2,1)S(1)}, u32[]{:S(2)}, u32[]{:S(2)}) collective-permute-start(bf16[256,768]{1,0:T(8,128)(2,1)S(1)} %slice.104), channel_id=1, source_target_pairs={{0,2},{2,0},{1,3},{3,1},{4,6},{6,4},{5,7},{7,5},{8,10},{10,8},{9,1... | collective-permute-start | bytes 1179656 | tf_op jit(solution)/shard_map/ppermute | solution.py:907
  148.2 23.1 %collective-permute-start.34 = (bf16[2,96,1536]{2,1,0:T(8,128)(2,1)S(1)}, bf16[2,96,1536]{2,1,0:T(8,128)(2,1)S(1)}, u32[]{:S(2)}, u32[]{:S(2)}) collective-permute-start(bf16[2,96,1536]{2,1,0:T(8,128)(2,1)S(1)} %dynamic-slice_bitcast_fusion.3), channel_id=1, source_target_pairs={{0,4},{4,0},{8,12},{12,8},{16,20},{20,16},{24,28},{28,24},{1,5},{5... | collective-permute-start | bytes 1769480 | tf_op jit(solution)/shard_map/ppermute | solution.py:907
  150.1 5.4 %collective-permute-start.16 = (bf16[256,768]{1,0:T(8,128)(2,1)S(1)}, bf16[256,768]{1,0:T(8,128)(2,1)S(1)}, u32[]{:S(2)}, u32[]{:S(2)}) collective-permute-start(bf16[256,768]{1,0:T(8,128)(2,1)S(1)} %add_convert_fusion.1.rows_mine), channel_id=1, source_target_pairs={{0,1},{1,0},{2,3},{3,2},{4,5},{5,4},{6,7},{7,6},{8,9},{9,8},{10,11... | collective-permute-start | bytes 1179656 | tf_op jit(solution)/shard_map/ppermute | solution.py:907
  150.3 5.2 %collective-permute-start.13 = (bf16[256,768]{1,0:T(8,128)(2,1)S(1)}, bf16[256,768]{1,0:T(8,128)(2,1)S(1)}, u32[]{:S(2)}, u32[]{:S(2)}) collective-permute-start(bf16[256,768]{1,0:T(8,128)(2,1)S(1)} %add_convert_fusion.2.out_mine), channel_id=1, source_target_pairs={{0,1},{1,0},{2,3},{3,2},{4,5},{5,4},{6,7},{7,6},{8,9},{9,8},{10,11... | collective-permute-start | bytes 1179656 | tf_op jit(solution)/shard_map/ppermute | solution.py:907
  155.2 40.4 %collective-permute-start.31 = (bf16[2,96,1536]{2,1,0:T(8,128)(2,1)S(1)}, bf16[2,96,1536]{2,1,0:T(8,128)(2,1)}, u32[]{:S(2)}, u32[]{:S(2)}) collective-permute-start(bf16[2,96,1536]{2,1,0:T(8,128)(2,1)S(1)} %dynamic-slice_bitcast_fusion.4), channel_id=1, source_target_pairs={{0,8},{4,12},{8,0},{12,4},{16,24},{20,28},{24,16},{28,20},{1,9},{5... | collective-permute-start | bytes 1769480 | tf_op jit(solution)/shard_map/ppermute | solution.py:907
  161.5 12.8 %collective-permute-start.17 = (bf16[512,192]{1,0:T(8,128)(2,1)S(1)}, bf16[512,192]{1,0:T(8,128)(2,1)S(1)}, u32[]{:S(2)}, u32[]{:S(2)}) collective-permute-start(bf16[512,192]{1,0:T(8,128)(2,1)S(1)} %get-tuple-element.56), channel_id=1, source_target_pairs={{0,2},{2,0},{1,3},{3,1},{4,6},{6,4},{5,7},{7,5},{8,10},{10,8},{9,1... | collective-permute-start | bytes 589832 | tf_op jit(solution)/shard_map/ppermute | solution.py:907
  171.5 13.4 %copy-start.15 = (bf16[2,96,1536]{2,1,0:T(8,128)(2,1)}, bf16[2,96,1536]{2,1,0:T(8,128)(2,1)S(1)}, u32[]{:S(2)}) copy-start(bf16[2,96,1536]{2,1,0:T(8,128)(2,1)S(1)} %fusion.6) | copy-start | bytes 1769476
  171.6 36.8 %collective-permute-start.35 = (bf16[96,1536]{1,0:T(8,128)(2,1)S(1)}, bf16[96,1536]{1,0:T(8,128)(2,1)}, u32[]{:S(2)}, u32[]{:S(2)}) collective-permute-start(bf16[96,1536]{1,0:T(8,128)(2,1)S(1)} %dynamic-slice_bitcast_fusion.6), channel_id=1, source_target_pairs={{0,16},{4,20},{8,24},{12,28},{16,0},{20,4},{24,8},{28,12},{1,17},{... | collective-permute-start | bytes 884744 | tf_op jit(solution)/shard_map/ppermute | solution.py:907
  174.2 12.2 %copy-start.12 = (bf16[768,576]{1,0:T(8,128)(2,1)S(1)}, bf16[768,576]{1,0:T(8,128)(2,1)}, u32[]{:S(2)}) copy-start(bf16[768,576]{1,0:T(8,128)(2,1)} %copy-done.11) | copy-start | bytes 2654212
  184.9 9.1 %collective-permute-start.26 = (f32[32,8]{1,0:T(8,128)S(1)}, f32[32,8]{1,0:T(8,128)S(1)}, u32[]{:S(2)}, u32[]{:S(2)}) collective-permute-start(f32[32,8]{1,0:T(8,128)S(1)} %bitcast.116), channel_id=1, source_target_pairs={{0,4},{4,0},{8,12},{12,8},{16,20},{20,16},{24,28},{28,24},{1,5},{5... | collective-permute-start | bytes 3080 | tf_op jit(solution)/shard_map/ppermute | solution.py:907
  193.5 18.0 %collective-permute-start.21 = (bf16[2,2,96,1024]{3,2,0,1:T(8,128)(2,1)}, bf16[2,2,96,1024]{3,2,0,1:T(8,128)(2,1)}, u32[]{:S(2)}, u32[]{:S(2)}) collective-permute-start(bf16[2,2,96,1024]{3,2,0,1:T(8,128)(2,1)} %bitcast.104), channel_id=1, source_target_pairs={{0,4},{4,0},{8,12},{12,8},{16,20},{20,16},{24,28},{28,24},{1,5},{5... | collective-permute-start | bytes 2359304 | tf_op jit(solution)/shard_map/ppermute | solution.py:907
  194.0 3.8 %collective-permute-start.27 = (f32[32,8]{1,0:T(8,128)S(1)}, f32[32,8]{1,0:T(8,128)S(1)}, u32[]{:S(2)}, u32[]{:S(2)}) collective-permute-start(f32[32,8]{1,0:T(8,128)S(1)} %slice_add_fusion.2), channel_id=1, source_target_pairs={{0,8},{4,12},{8,0},{12,4},{16,24},{20,28},{24,16},{28,20},{1,9},{5... | collective-permute-start | bytes 3080 | tf_op jit(solution)/shard_map/ppermute | solution.py:907
  197.8 6.1 %collective-permute-start.28 = (f32[32,8]{1,0:T(8,128)S(1)}, f32[32,8]{1,0:T(8,128)S(1)}, u32[]{:S(2)}, u32[]{:S(2)}) collective-permute-start(f32[32,8]{1,0:T(8,128)S(1)} %add.164), channel_id=1, source_target_pairs={{0,16},{4,20},{8,24},{12,28},{16,0},{20,4},{24,8},{28,12},{1,17},{... | collective-permute-start | bytes 3080 | tf_op jit(solution)/shard_map/ppermute | solution.py:907
  198.9 12.5 %copy-start.14 = (bf16[2,2,1,96,1024]{4,3,2,1,0:T(8,128)(2,1)S(1)}, bf16[2,2,1,96,1024]{4,3,2,1,0:T(8,128)(2,1)}, u32[]{:S(2)}) copy-start(bf16[2,2,1,96,1024]{4,3,2,1,0:T(8,128)(2,1)} %get-tuple-element.140) | copy-start | bytes 2359300
  198.9 17.6 %collective-permute-start.32 = (bf16[96,1536]{1,0:T(8,128)(2,1)}, bf16[96,1536]{1,0:T(8,128)(2,1)}, u32[]{:S(2)}, u32[]{:S(2)}) collective-permute-start(bf16[96,1536]{1,0:T(8,128)(2,1)} %dynamic-slice_bitcast_fusion.7), channel_id=1, source_target_pairs={{0,16},{4,20},{8,24},{12,28},{16,0},{20,4},{24,8},{28,12},{1,17},{... | collective-permute-start | bytes 884744 | tf_op jit(solution)/shard_map/ppermute | solution.py:907
  204.0 3.7 %collective-permute-start.29 = (f32[32,8]{1,0:T(8,128)S(1)}, f32[32,8]{1,0:T(8,128)S(1)}, u32[]{:S(2)}, u32[]{:S(2)}) collective-permute-start(f32[32,8]{1,0:T(8,128)S(1)} %add.165), channel_id=1, source_target_pairs={{0,2},{2,0},{1,3},{3,1},{4,6},{6,4},{5,7},{7,5},{8,10},{10,8},{9,1... | collective-permute-start | bytes 3080 | tf_op jit(solution)/shard_map/ppermute | solution.py:907
  205.4 9.2 %collective-permute-start.18 = (bf16[512,768]{1,0:T(8,128)(2,1)}, bf16[512,768]{1,0:T(8,128)(2,1)}, u32[]{:S(2)}, u32[]{:S(2)}) collective-permute-start(bf16[512,768]{1,0:T(8,128)(2,1)} %dynamic-slice_bitcast_fusion), channel_id=1, source_target_pairs={{0,1},{1,0},{2,3},{3,2},{4,5},{5,4},{6,7},{7,6},{8,9},{9,8},{10,11... | collective-permute-start | bytes 2359304 | tf_op jit(solution)/shard_map/ppermute | solution.py:907
  212.9 8.4 %collective-permute-start.22 = (bf16[2,96,1024]{2,1,0:T(8,128)(2,1)S(1)}, bf16[2,96,1024]{2,1,0:T(8,128)(2,1)S(1)}, u32[]{:S(2)}, u32[]{:S(2)}) collective-permute-start(bf16[2,96,1024]{2,1,0:T(8,128)(2,1)S(1)} %dynamic-slice_bitcast_fusion.5), channel_id=1, source_target_pairs={{0,8},{4,12},{8,0},{12,4},{16,24},{20,28},{24,16},{28,20},{1,9},{5... | collective-permute-start | bytes 1179656 | tf_op jit(solution)/shard_map/ppermute | solution.py:907
  215.9 8.1 %collective-permute-start.19 = (bf16[256,768]{1,0:T(8,128)(2,1)S(1)}, bf16[256,768]{1,0:T(8,128)(2,1)S(1)}, u32[]{:S(2)}, u32[]{:S(2)}) collective-permute-start(bf16[256,768]{1,0:T(8,128)(2,1)S(1)} %slice.108), channel_id=1, source_target_pairs={{0,2},{2,0},{1,3},{3,1},{4,6},{6,4},{5,7},{7,5},{8,10},{10,8},{9,1... | collective-permute-start | bytes 1179656 | tf_op jit(solution)/shard_map/ppermute | solution.py:907
  221.5 8.7 %collective-permute-start.23 = (bf16[96,1024]{1,0:T(8,128)(2,1)S(1)}, bf16[96,1024]{1,0:T(8,128)(2,1)S(1)}, u32[]{:S(2)}, u32[]{:S(2)}) collective-permute-start(bf16[96,1024]{1,0:T(8,128)(2,1)S(1)} %dynamic-slice_bitcast_fusion.8), channel_id=1, source_target_pairs={{0,16},{4,20},{8,24},{12,28},{16,0},{20,4},{24,8},{28,12},{1,17},{... | collective-permute-start | bytes 589832 | tf_op jit(solution)/shard_map/ppermute | solution.py:907
  224.1 14.5 %copy-start.2 = (f32[512,768]{1,0:T(8,128)S(1)}, f32[512,768]{1,0:T(8,128)}, u32[]{:S(2)}) copy-start(f32[512,768]{1,0:T(8,128)} %get-tuple-element.54.grad_hidden) | copy-start | bytes 4718596
  224.1 14.5 %collective-permute-start.20 = (bf16[256,768]{1,0:T(8,128)(2,1)S(1)}, bf16[256,768]{1,0:T(8,128)(2,1)S(1)}, u32[]{:S(2)}, u32[]{:S(2)}) collective-permute-start(bf16[256,768]{1,0:T(8,128)(2,1)S(1)} %add_convert_fusion.mine), channel_id=1, source_target_pairs={{0,1},{1,0},{2,3},{3,2},{4,5},{5,4},{6,7},{7,6},{8,9},{9,8},{10,11... | collective-permute-start | bytes 1179656 | tf_op jit(solution)/shard_map/ppermute | solution.py:907
  230.3 4.7 %collective-permute-start.24 = (bf16[48,1024]{1,0:T(8,128)(2,1)S(1)}, bf16[48,1024]{1,0:T(8,128)(2,1)S(1)}, u32[]{:S(2)}, u32[]{:S(2)}) collective-permute-start(bf16[48,1024]{1,0:T(8,128)(2,1)S(1)} %get-tuple-element.148), channel_id=1, source_target_pairs={{0,2},{2,0},{1,3},{3,1},{4,6},{6,4},{5,7},{7,5},{8,10},{10,8},{9,1... | collective-permute-start | bytes 294920 | tf_op jit(solution)/shard_map/ppermute | solution.py:907
  235.8 2.3 collective-permute-start.25
  (13 other events, 53.5 us)
